TPU v7x, 768 devices: a whole 4x8x12 slice. The times are simulated.
768 devices in a mesh: comp: 2 (over z_hi), col: 384 (over x, y, z_lo, core).
Axes of the slice: x: 4, y: 8, z: 12 (z_hi: 2, z_lo: 6; z = z_hi * 6 + z_lo), core: 2. Of those that a mesh axis runs over, the one named last changes fastest.
Arguments:
- column_state: float32 [2, 2, 80, 786432], P('comp', None, None, 'col'), may hold values from -6 to 6
- neighbour_offsets: int32 [2, 6, 786432], P('comp', None, 'col'), may hold values from -256 to 256
- edge_coefficients: float32 [2, 6, 786432], P('comp', None, 'col'), may hold values from 0.02 to 0.15
- active_levels: int32 [2, 786432], P('comp', 'col'), may hold values from 0 to 80, as said below
- intersection_offsets: int32 [2, 8, 786432], P('comp', None, 'col'), may hold values from -256 to 256, as said below
- intersection_weights: float32 [2, 8, 786432], P('comp', None, 'col'), may hold values from 0 to 1, as said below
- relaxation: float32 [2, 2], P('comp'), may hold values from 0.2 to 0.6
Outputs:
- coupled_state: float32 [2, 2, 80, 786432], P('comp', None, None, 'col')
- remapped: float32 [2, 2, 786432], P('comp', None, 'col')
Inputs may be any that keep to these rules, and one draw needn't show every extreme that they name: `active_levels`: atmosphere columns have 72 active levels; ocean columns 0 on land, else 8 or more. `intersection_offsets`: each intersection source lies within 256 columns of the destination's position in the other component's order. `intersection_weights`: each destination column has 1 to 8 used intersection slots, the first ones; unused slots have weight 0.
All inputs are finite; a program needn't handle non-finite values.
Results may differ from a plain program's by a relative error of at most 0.00008.
Values sent between devices are 32-bit elements; how exact they have to be, the bound alone decides.
No kernel may reach another device: no remote copies, remote signals or barrier semaphores. Data moves between devices by JAX's collectives and lax.ppermute only.
A program may use at most 32 MiB of HBM per device.

v0:
```python
import math

import jax
import jax.numpy as jnp
from jax import lax
from jax.sharding import PartitionSpec as P


def extended_2(array, sides, width):
    for axis, dim in sides:
        size, length = (lax.axis_size(axis), array.shape[dim])
        up = [(i, (i + 1) % size) for i in range(size - 1)]
        down = [(j, i) for i, j in up]
        last = lax.slice_in_dim(array, length - width, length, axis=dim)
        initial = lax.slice_in_dim(array, 0, width, axis=dim)
        before = lax.ppermute(last, axis, up)
        after = lax.ppermute(initial, axis, down)
        array = jnp.concatenate([before, array, after], axis=dim)
    return array


def swapped(value, axis, distance):
    mask = 2**distance
    pairs = [(source, source ^ mask) for source in range(lax.axis_size(axis))]
    return lax.ppermute(value, axis, pairs)


def band_apply(extended, start, columns, offsets, weights, reach):
    width = extended.shape[-1]
    source_rows = extended.reshape(-1, width)
    row_count = source_rows.shape[0]
    block = math.gcd(columns, 128)
    window = block + 2 * reach
    count = columns // block
    local = jnp.arange(window, dtype=jnp.int32)[None, :, None]
    inner = jnp.arange(block, dtype=jnp.int32)[None, None, :]
    flat_offsets = offsets[0]
    flat_weights = weights[0]

    def one_block(index, result):
        first = index * block
        block_offsets = lax.dynamic_slice_in_dim(flat_offsets, first, block, 1)
        block_weights = lax.dynamic_slice_in_dim(flat_weights, first, block, 1)
        source = lax.dynamic_slice_in_dim(source_rows, start + first - reach, window, 1)
        hits = local == block_offsets[:, None, :] + reach + inner
        table = jnp.sum(jnp.where(hits, block_weights[:, None, :], 0.0), axis=0)
        product = jnp.dot(
            source, table, precision=lax.Precision.HIGHEST, preferred_element_type=jnp.float32
        )
        return lax.dynamic_update_slice_in_dim(result, product, first, 1)

    result = jnp.zeros((row_count, columns), jnp.float32)
    result = lax.fori_loop(0, count, one_block, result)
    return result.reshape(extended.shape[:-1] + (columns,))


def relax_columns(extended, start, columns, offsets, coefficients, active, reach):
    centre = lax.slice_in_dim(extended, start, start + columns, axis=3)
    gathered = band_apply(extended, start, columns, offsets, coefficients, reach)
    total = jnp.sum(coefficients, axis=1)
    summed = gathered - total[:, None, None, :] * centre
    levels = jnp.arange(centre.shape[2], dtype=jnp.int32)[:, None]
    wet_mask = (levels < active[:, None, None, :]).astype(jnp.float32)
    return centre + wet_mask * summed


def body(
    column_state,
    neighbour_offsets,
    edge_coefficients,
    active_levels,
    intersection_offsets,
    intersection_weights,
    relaxation,
):
    columns = column_state.shape[3]
    rim_width = columns // 8
    advanced = column_state
    for substep in range(2):
        extended = extended_2(advanced, (("col", 3),), rim_width)
        advanced = relax_columns(
            extended,
            rim_width,
            columns,
            neighbour_offsets,
            edge_coefficients,
            active_levels,
            rim_width,
        )
    partner_surface = swapped(column_state[:, :, 0, :], "comp", 0)
    partner_ext = extended_2(partner_surface, (("col", 2),), rim_width)
    remapped = band_apply(
        partner_ext, rim_width, columns, intersection_offsets, intersection_weights, rim_width
    )
    levels = jnp.arange(column_state.shape[2], dtype=jnp.int32)[:, None]
    surface_mask = ((levels == 0) & (levels < active_levels[:, None, None, :])).astype(jnp.float32)
    coupled_state = advanced + surface_mask * (
        relaxation[:, :, None, None] * (remapped[:, :, None, :] - advanced)
    )
    return (coupled_state, remapped)


def solution(mesh):
    return jax.shard_map(
        body,
        mesh=mesh,
        in_specs=(
            P("comp", None, None, "col"),
            P("comp", None, "col"),
            P("comp", None, "col"),
            P("comp", "col"),
            P("comp", None, "col"),
            P("comp", None, "col"),
            P("comp", None),
        ),
        out_specs=(P("comp", None, None, "col"), P("comp", None, "col")),
        check_vma=False,
    )
```

profile of v0, /device:TPU:6, one launch (start us, length us, event | category | flops | bytes accessed | tf_op | source)
XLA Modules:
  0.0 149.7 jit_solution(5221990979845845556)
XLA Ops:
  0.7 1.1 fusion.22
  1.8 1.9 %collective-permute-start = (f32[1,2,80,256]{3,2,1,0:T(8,128)S(1)}, f32[1,2,80,256]{3,2,1,0:T(8,128)S(1)}, u32[]{:S(2)}, u32[]{:S(2)}) collective-permute-start(f32[1,2,80,256]{3,2,1,0:T(8,128)S(1)} %get-tuple-element.760), channel_id=1, source_target_pairs={{0,1},{1,2},{2,3},{3,4},{4,5},{5,6},{6,7},{7,8},{8,9},{9,10},{10,1... | collective-permute-start | bytes 491528 | tf_op jit(solution)/shard_map/ppermute | solution.py:16
  3.7 15.3 %collective-permute-start.1 = (f32[1,2,80,256]{3,2,1,0:T(8,128)S(1)}, f32[1,2,80,256]{3,2,1,0:T(8,128)}, u32[]{:S(2)}, u32[]{:S(2)}) collective-permute-start(f32[1,2,80,256]{3,2,1,0:T(8,128)S(1)} %get-tuple-element.761), channel_id=1, source_target_pairs={{1,0},{2,1},{3,2},{4,3},{5,4},{6,5},{7,6},{8,7},{9,8},{10,9},{11,1... | collective-permute-start | bytes 491528 | tf_op jit(solution)/shard_map/ppermute | solution.py:17
  19.1 0.9 slice.25
  20.0 11.3 %collective-permute-start.4 = (f32[1,2,2048]{2,1,0:T(2,128)S(1)}, f32[1,2,2048]{2,1,0:T(2,128)S(1)}, u32[]{:S(2)}, u32[]{:S(2)}) collective-permute-start(f32[1,2,2048]{2,1,0:T(2,128)S(1)} %bitcast.36), channel_id=1, source_target_pairs={{0,384},{384,0},{1,385},{385,1},{2,386},{386,2},{3,387},{387,3},{4... | collective-permute-start | bytes 49160 | tf_op jit(solution)/shard_map/ppermute | solution.py:25
  31.3 1.7 %collective-permute-done.4 = f32[1,2,2048]{2,1,0:T(2,128)S(1)} collective-permute-done((f32[1,2,2048]{2,1,0:T(2,128)S(1)}, f32[1,2,2048]{2,1,0:T(2,128)S(1)}, u32[]{:S(2)}, u32[]{:S(2)}) %collective-permute-start.4) | collective-permute-done | bytes 16416 | tf_op jit(solution)/shard_map/ppermute | solution.py:25
  33.0 1.9 %collective-permute-start.5 = (f32[1,2,256]{2,1,0:T(2,128)S(1)}, f32[1,2,256]{2,1,0:T(2,128)S(1)}, u32[]{:S(2)}, u32[]{:S(2)}) collective-permute-start(f32[1,2,256]{2,1,0:T(2,128)S(1)} %get-tuple-element.762), channel_id=1, source_target_pairs={{0,1},{1,2},{2,3},{3,4},{4,5},{5,6},{6,7},{7,8},{8,9},{9,10},{10,1... | collective-permute-start | bytes 6152 | tf_op jit(solution)/shard_map/ppermute | solution.py:16
  34.9 11.5 %collective-permute-start.6 = (f32[1,2,256]{2,1,0:T(2,128)S(1)}, f32[1,2,256]{2,1,0:T(2,128)S(1)}, u32[]{:S(2)}, u32[]{:S(2)}) collective-permute-start(f32[1,2,256]{2,1,0:T(2,128)S(1)} %get-tuple-element.763), channel_id=1, source_target_pairs={{1,0},{2,1},{3,2},{4,3},{5,4},{6,5},{7,6},{8,7},{9,8},{10,9},{11,1... | collective-permute-start | bytes 6152 | tf_op jit(solution)/shard_map/ppermute | solution.py:17
  46.3 1.8 %fusion.20 = (f32[80,2048]{1,0:T(8,128)}, f32[80,2048]{1,0:T(8,128)}) fusion(s32[2048]{0:T(1024)} %bitcast.37, pred[80]{0:T(512)(128)(4,1)S(1)} %iota_compare_fusion.4), kind=kLoop, calls=%fused_computation.34 | loop fusion | flops 655360 | bytes 1318992 | tf_op jit(solution)/shard_map/convert_element_type | solution.py:96
  48.4 1.0 pad_maximum_fusion
  49.4 1.2 broadcast.134.clone
  50.6 22.7 %while.54 = (s32[]{:T(128)}, f32[160,2048]{1,0:T(8,128)}, f32[160,2560]{1,0:T(8,128)S(1)}, s32[6,2048]{1,0:T(8,128)S(1)}, f32[6,2048]{1,0:T(8,128)S(1)}, /*index...) while((s32[]{:T(128)}, f32[160,2048]{1,0:T(8,128)}, f32[160,2560]{1,0:T(8,128)S(1)}, ...), condition=%wide.region_2.3_spmd.clone, body=%wide.region_0.2_spmd.clone.sunk | while | flops 158680576 | bytes 1165500 | solution.py:53
  50.9 1.2 convolution_dynamic-update-slice_fusion.6
  52.3 1.2 convolution_dynamic-update-slice_fusion.6
  53.7 1.2 convolution_dynamic-update-slice_fusion.6
  55.1 1.2 convolution_dynamic-update-slice_fusion.6
  56.6 1.2 convolution_dynamic-update-slice_fusion.6
  58.0 1.2 convolution_dynamic-update-slice_fusion.6
  59.4 1.2 convolution_dynamic-update-slice_fusion.6
  60.8 1.2 convolution_dynamic-update-slice_fusion.6
  62.3 1.2 convolution_dynamic-update-slice_fusion.6
  63.7 1.2 convolution_dynamic-update-slice_fusion.6
  65.1 1.2 convolution_dynamic-update-slice_fusion.6
  66.5 1.2 convolution_dynamic-update-slice_fusion.6
  67.9 1.2 convolution_dynamic-update-slice_fusion.6
  69.4 1.2 convolution_dynamic-update-slice_fusion.6
  70.8 1.2 convolution_dynamic-update-slice_fusion.6
  72.2 1.2 convolution_dynamic-update-slice_fusion.6
  73.4 1.7 %multiply_add_fusion.1 = f32[1,2,80,2048]{3,2,1,0:T(8,128)S(1)} fusion(f32[1,2,80,2048]{3,2,1,0:T(8,128)S(1)} %copy-done, f32[1,2,80,2048]{3,2,1,0:T(8,128)} %bitcast.32, f32[2048]{0:T(1024)S(1)} %reduce_sum.70, f32[80,2048]{1,0:T(8,128)} %get-tuple-element.765), kind=kLoop, calls=%fused_computation.30 | loop fusion | flops 1310720 | bytes 4595712 | tf_op jit(solution)/shard_map/add | solution.py:64
  75.1 1.9 %collective-permute-start.2 = (f32[1,2,80,256]{3,2,1,0:T(8,128)S(1)}, f32[1,2,80,256]{3,2,1,0:T(8,128)S(1)}, u32[]{:S(2)}, u32[]{:S(2)}) collective-permute-start(f32[1,2,80,256]{3,2,1,0:T(8,128)S(1)} %get-tuple-element.758), channel_id=1, source_target_pairs={{0,1},{1,2},{2,3},{3,4},{4,5},{5,6},{6,7},{7,8},{8,9},{9,10},{10,1... | collective-permute-start | bytes 491528 | tf_op jit(solution)/shard_map/ppermute | solution.py:16
  77.1 11.5 %collective-permute-start.3 = (f32[1,2,80,256]{3,2,1,0:T(8,128)S(1)}, f32[1,2,80,256]{3,2,1,0:T(8,128)}, u32[]{:S(2)}, u32[]{:S(2)}) collective-permute-start(f32[1,2,80,256]{3,2,1,0:T(8,128)S(1)} %get-tuple-element.759), channel_id=1, source_target_pairs={{1,0},{2,1},{3,2},{4,3},{5,4},{6,5},{7,6},{8,7},{9,8},{10,9},{11,1... | collective-permute-start | bytes 491528 | tf_op jit(solution)/shard_map/ppermute | solution.py:17
  88.6 32.2 %while.56 = (s32[]{:T(128)}, f32[2,2048]{1,0:T(2,128)S(1)}, f32[2,2560]{1,0:T(2,128)S(1)}, s32[8,2048]{1,0:T(8,128)}, f32[8,2048]{1,0:T(8,128)}, /*index=5*/s32[...) while((s32[]{:T(128)}, f32[2,2048]{1,0:T(2,128)S(1)}, f32[2,2560]{1,0:T(2,128)S(1)}, ...), condition=%wide.region_9.10_spmd.clone, body=%wide.region_7.0_spmd.clone.sunk | while | flops 3852296 | bytes 686268 | solution.py:53
  90.6 0.7 constant_dynamic-slice_fusion.8
  92.6 0.7 constant_dynamic-slice_fusion.8
  94.6 0.7 constant_dynamic-slice_fusion.8
  98.6 0.7 constant_dynamic-slice_fusion.8
  100.6 0.7 constant_dynamic-slice_fusion.8
  102.6 0.7 constant_dynamic-slice_fusion.8
  104.6 0.7 constant_dynamic-slice_fusion.8
  106.7 0.7 constant_dynamic-slice_fusion.8
  108.7 0.7 constant_dynamic-slice_fusion.8
  110.7 0.7 constant_dynamic-slice_fusion.8
  112.7 0.7 constant_dynamic-slice_fusion.8
  114.7 0.7 constant_dynamic-slice_fusion.8
  121.4 1.1 pad_maximum_fusion.1
  122.5 1.2 broadcast.134
  123.7 22.7 %while.55 = (s32[]{:T(128)}, f32[160,2048]{1,0:T(8,128)}, f32[160,2560]{1,0:T(8,128)S(1)}, s32[6,2048]{1,0:T(8,128)S(1)}, f32[6,2048]{1,0:T(8,128)S(1)}, /*index...) while((s32[]{:T(128)}, f32[160,2048]{1,0:T(8,128)}, f32[160,2560]{1,0:T(8,128)S(1)}, ...), condition=%wide.region_6.7_spmd.clone, body=%wide.region_4.6_spmd.clone.sunk | while | flops 158680576 | bytes 1165500 | solution.py:53
  124.0 1.2 convolution_dynamic-update-slice_fusion.7
  125.4 1.2 convolution_dynamic-update-slice_fusion.7
  126.8 1.2 convolution_dynamic-update-slice_fusion.7
  128.3 1.2 convolution_dynamic-update-slice_fusion.7
  129.7 1.2 convolution_dynamic-update-slice_fusion.7
  131.1 1.2 convolution_dynamic-update-slice_fusion.7
  132.5 1.2 convolution_dynamic-update-slice_fusion.7
  133.9 1.2 convolution_dynamic-update-slice_fusion.7
  135.4 1.2 convolution_dynamic-update-slice_fusion.7
  136.8 1.2 convolution_dynamic-update-slice_fusion.7
  138.2 1.2 convolution_dynamic-update-slice_fusion.7
  139.6 1.2 convolution_dynamic-update-slice_fusion.7
  141.1 1.2 convolution_dynamic-update-slice_fusion.7
  142.5 1.2 convolution_dynamic-update-slice_fusion.7
  143.9 1.2 convolution_dynamic-update-slice_fusion.7
  145.3 1.2 convolution_dynamic-update-slice_fusion.7
  146.5 3.2 %multiply_add_fusion = f32[1,2,80,2048]{3,2,1,0:T(8,128)} fusion(f32[1,2,80,2048]{3,2,1,0:T(8,128)S(1)} %multiply_add_fusion.1, f32[1,2,80,2048]{3,2,1,0:T(8,128)} %bitcast.31, f32[2,2048]{1,0:T(2,128)S(1)} %get-tuple-element.688, f32[2]{0:T(128)S(1)} %bitcast.40, f32[80,2048]{1,0:T(8,128)} %get-tuple-element.764, f32[2048]{0:T(1024)S(1)} %reduce_sum.70, ...), kind=kLoop, calls=%fused_computation.29 | loop fusion | flops 2621440 | bytes 5267464 | tf_op jit(solution)/shard_map/add | solution.py:97
  (175 shorter events, 32.2 us)
Async XLA Ops:
  0.6 47.7 %copy-start = (f32[1,2,80,2048]{3,2,1,0:T(8,128)S(1)}, f32[1,2,80,2048]{3,2,1,0:T(8,128)}, u32[]{:S(2)}) copy-start(f32[1,2,80,2048]{3,2,1,0:T(8,128)} %param.13) | copy-start | bytes 3932164
  0.6 47.6 %copy-start.1 = (f32[1,6,2048]{2,0,1:T(1,128)S(1)}, f32[1,6,2048]{2,0,1:T(1,128)}, u32[]{:S(2)}) copy-start(f32[1,6,2048]{2,0,1:T(1,128)} %param.15) | copy-start | bytes 147460
  0.7 47.6 %copy-start.4 = (s32[1,6,2048]{2,0,1:T(1,128)S(1)}, s32[1,6,2048]{2,0,1:T(1,128)}, u32[]{:S(2)}) copy-start(s32[1,6,2048]{2,0,1:T(1,128)} %param.14) | copy-start | bytes 147460
  1.8 46.6 %collective-permute-start = (f32[1,2,80,256]{3,2,1,0:T(8,128)S(1)}, f32[1,2,80,256]{3,2,1,0:T(8,128)S(1)}, u32[]{:S(2)}, u32[]{:S(2)}) collective-permute-start(f32[1,2,80,256]{3,2,1,0:T(8,128)S(1)} %get-tuple-element.760), channel_id=1, source_target_pairs={{0,1},{1,2},{2,3},{3,4},{4,5},{5,6},{6,7},{7,8},{8,9},{9,10},{10,1... | collective-permute-start | bytes 491528 | tf_op jit(solution)/shard_map/ppermute | solution.py:16
  3.7 44.7 %collective-permute-start.1 = (f32[1,2,80,256]{3,2,1,0:T(8,128)S(1)}, f32[1,2,80,256]{3,2,1,0:T(8,128)}, u32[]{:S(2)}, u32[]{:S(2)}) collective-permute-start(f32[1,2,80,256]{3,2,1,0:T(8,128)S(1)} %get-tuple-element.761), channel_id=1, source_target_pairs={{1,0},{2,1},{3,2},{4,3},{5,4},{6,5},{7,6},{8,7},{9,8},{10,9},{11,1... | collective-permute-start | bytes 491528 | tf_op jit(solution)/shard_map/ppermute | solution.py:17
  20.0 13.0 %collective-permute-start.4 = (f32[1,2,2048]{2,1,0:T(2,128)S(1)}, f32[1,2,2048]{2,1,0:T(2,128)S(1)}, u32[]{:S(2)}, u32[]{:S(2)}) collective-permute-start(f32[1,2,2048]{2,1,0:T(2,128)S(1)} %bitcast.36), channel_id=1, source_target_pairs={{0,384},{384,0},{1,385},{385,1},{2,386},{386,2},{3,387},{387,3},{4... | collective-permute-start | bytes 49160 | tf_op jit(solution)/shard_map/ppermute | solution.py:25
  33.0 15.3 %collective-permute-start.5 = (f32[1,2,256]{2,1,0:T(2,128)S(1)}, f32[1,2,256]{2,1,0:T(2,128)S(1)}, u32[]{:S(2)}, u32[]{:S(2)}) collective-permute-start(f32[1,2,256]{2,1,0:T(2,128)S(1)} %get-tuple-element.762), channel_id=1, source_target_pairs={{0,1},{1,2},{2,3},{3,4},{4,5},{5,6},{6,7},{7,8},{8,9},{9,10},{10,1... | collective-permute-start | bytes 6152 | tf_op jit(solution)/shard_map/ppermute | solution.py:16
  34.9 13.4 %collective-permute-start.6 = (f32[1,2,256]{2,1,0:T(2,128)S(1)}, f32[1,2,256]{2,1,0:T(2,128)S(1)}, u32[]{:S(2)}, u32[]{:S(2)}) collective-permute-start(f32[1,2,256]{2,1,0:T(2,128)S(1)} %get-tuple-element.763), channel_id=1, source_target_pairs={{1,0},{2,1},{3,2},{4,3},{5,4},{6,5},{7,6},{8,7},{9,8},{10,9},{11,1... | collective-permute-start | bytes 6152 | tf_op jit(solution)/shard_map/ppermute | solution.py:17
  75.1 45.6 %collective-permute-start.2 = (f32[1,2,80,256]{3,2,1,0:T(8,128)S(1)}, f32[1,2,80,256]{3,2,1,0:T(8,128)S(1)}, u32[]{:S(2)}, u32[]{:S(2)}) collective-permute-start(f32[1,2,80,256]{3,2,1,0:T(8,128)S(1)} %get-tuple-element.758), channel_id=1, source_target_pairs={{0,1},{1,2},{2,3},{3,4},{4,5},{5,6},{6,7},{7,8},{8,9},{9,10},{10,1... | collective-permute-start | bytes 491528 | tf_op jit(solution)/shard_map/ppermute | solution.py:16
  77.1 44.3 %collective-permute-start.3 = (f32[1,2,80,256]{3,2,1,0:T(8,128)S(1)}, f32[1,2,80,256]{3,2,1,0:T(8,128)}, u32[]{:S(2)}, u32[]{:S(2)}) collective-permute-start(f32[1,2,80,256]{3,2,1,0:T(8,128)S(1)} %get-tuple-element.759), channel_id=1, source_target_pairs={{1,0},{2,1},{3,2},{4,3},{5,4},{6,5},{7,6},{8,7},{9,8},{10,9},{11,1... | collective-permute-start | bytes 491528 | tf_op jit(solution)/shard_map/ppermute | solution.py:17
  120.7 25.8 %copy-start.3 = (f32[2,2048]{1,0:T(2,128)}, f32[2,2048]{1,0:T(2,128)S(1)}, u32[]{:S(2)}) copy-start(f32[2,2048]{1,0:T(2,128)S(1)} %get-tuple-element.688) | copy-start | bytes 49156
  120.7 0.7 copy-start.2
  123.7 22.8 %copy-start.5 = (f32[1,2]{1,0:T(1,128)S(1)}, f32[1,2]{1,0:T(1,128)}, u32[]{:S(2)}) copy-start(f32[1,2]{1,0:T(1,128)} %param.19) | copy-start | bytes 28
where the time goes:
time: 151 us; the launch traced here: 150 us
  starting transfers between devices  55.3 us (37%)
  matrix products  42 us (28%)
  other arithmetic  32.9 us (22%)
  local copies, waits for them, and re-layouts  16.5 us (11%)
  waiting for transfers between devices  1.71 us (1%)
    dot_general x48, matrix products, one_block(): jnp.dot(source, table, precision=lax.Precision.HIGHEST, preferred_element...  42 us
    ppermute x3, starting transfers between devices, extended_2(): after = lax.ppermute(initial, axis, down)  38.3 us
    reduce_sum x48, other arithmetic, one_block(): table = jnp.sum(jnp.where(hits, block_weights[:, None, :], 0.0), axis=0)  12.7 us
    dynamic_slice x48, local copies, waits for them, and re-layouts, one_block(): block_weights = lax.dynamic_slice_in_dim(flat_weights, first, block, 1)  11.3 us
    ppermute x1, starting transfers between devices, swapped(): return lax.ppermute(value, axis, pairs)  11.3 us
    add x48, other arithmetic, one_block(): hits = local == block_offsets[:, None, :] + reach + inner  11.2 us
    ppermute x3, starting transfers between devices, extended_2(): before = lax.ppermute(last, axis, up)  5.75 us
    add x1, other arithmetic, body(): advanced + surface_mask * (relaxation[:, :, None, None] * (remapped[:, :,...  3.18 us
  transfers between devices with their start and end apart: 7, of which 1 were waited for; matrix products, arithmetic and copies ran while one was open for 23% of the time, Pallas kernels for 0%

commit v1 on v0

v1 whole, which is shorter than its diff:
```python
import functools

import jax
import jax.numpy as jnp
from jax import lax
from jax.experimental import pallas as pl
from jax.experimental.pallas import tpu as pltpu
from jax.sharding import PartitionSpec as P

NF = 2
LEV = 80
ROWS = NF * LEV
COLS = 2048
HALO = 256
EDGE = 2 * HALO
KN = 6
KR = 8
BLOCK = 256
WINDOW = BLOCK + 2 * HALO
MID = COLS + 2 * HALO
SENT = ROWS + 8
LANES = 128
PANEL = 16
PACK_MIB = 60
RUN = 12

ANY = pl.BlockSpec(memory_space=pl.ANY)
HBM = pl.BlockSpec(memory_space=pltpu.HBM)
VMEM = pl.BlockSpec(memory_space=pltpu.VMEM)


def params(mib):
    return pltpu.CompilerParams(vmem_limit_bytes=mib << 20)


def on_first_core():
    return lax.rem(lax.axis_index("col"), 2) == 0


def pack_kernel(state, off_in, coef_in, act_in, beside, chip, surf, tiles, off, coef, act, sems):
    first = on_first_core()
    lists = [
        pltpu.make_async_copy(source, target, sems.at[4 + at])
        for at, (source, target) in enumerate(((off_in, off), (coef_in, coef), (act_in, act)))
    ]
    rows = [
        pltpu.make_async_copy(state.at[pl.ds(LEV * field, 8), :], tiles.at[field], sems.at[2 + field])
        for field in range(NF)
    ]

    def send(out, high, at):
        start = COLS - EDGE if high else 0
        copy = pltpu.make_async_copy(state.at[:, pl.ds(start, EDGE)], out.at[pl.ds(0, ROWS), :], sems.at[at])
        copy.start()
        return copy

    def fill(out, high):
        out[ROWS + KN : SENT, :] = jnp.zeros((8 - KN, EDGE), jnp.float32)
        for part in range(HALO // LANES):
            j = (COLS - HALO if high else 0) // LANES + part
            here = slice(part * LANES, (part + 1) * LANES)
            there = slice(HALO + part * LANES, HALO + (part + 1) * LANES)
            for k in range(KN):
                out[ROWS + k : ROWS + k + 1, here] = off[k, j : j + 1, :].astype(jnp.float32)
                out[ROWS + k : ROWS + k + 1, there] = coef[k, j : j + 1, :]
            out[ROWS + KN : ROWS + KN + 1, here] = act[:, j * LANES : (j + 1) * LANES].astype(jnp.float32)

    def both(high):
        copies = [send(beside, high, 0), send(chip, not high, 1)] + rows
        for copy in lists + rows:
            copy.start()
        for copy in lists:
            copy.wait()
        fill(beside, high)
        fill(chip, not high)
        for copy in copies:
            copy.wait()

    @pl.when(first)
    def _():
        both(False)

    @pl.when(jnp.logical_not(first))
    def _():
        both(True)

    for field in range(NF):
        surf[field : field + 1, :] = tiles[field, 0:1, :]


def pack(state, off, coef, act):
    sent = jax.ShapeDtypeStruct((SENT, EDGE), jnp.float32)
    return pl.pallas_call(
        pack_kernel,
        out_shape=(sent, sent, jax.ShapeDtypeStruct((NF, COLS), jnp.float32)),
        in_specs=[HBM, HBM, HBM, HBM],
        out_specs=(VMEM, VMEM, VMEM),
        scratch_shapes=[
            pltpu.VMEM((NF, 8, COLS), jnp.float32),
            pltpu.VMEM(off.shape, off.dtype),
            pltpu.VMEM(coef.shape, coef.dtype),
            pltpu.VMEM(act.shape, act.dtype),
            pltpu.SemaphoreType.DMA((7,)),
        ],
        compiler_params=params(PACK_MIB),
        name="pack",
    )(state, off, coef, act)


def from_far():
    place = lax.rem(lax.axis_index("col"), RUN)
    return jnp.logical_or(place == 0, place == RUN - 1)


def widen_kernel(chip, near, far, surf, out, tiles, sems):
    first = on_first_core()

    def bring(source, left, at):
        start = HALO if left else 0
        copies = [
            pltpu.make_async_copy(
                source.at[pl.ds(LEV * field, 8), pl.ds(start, HALO)],
                tiles.at[0 if left else 1, field],
                sems.at[NF * at + field],
            )
            for field in range(NF)
        ]
        for copy in copies:
            copy.start()
        return copies

    def both(source, left):
        for copy in bring(source, left, 0) + bring(chip, not left, 1):
            copy.wait()

    for source, is_far in ((far, True), (near, False)):
        for left in (True, False):

            @pl.when(jnp.logical_and(from_far() == is_far, first == left))
            def _(source=source, left=left):
                both(source, left)

    out[:, HALO : HALO + COLS] = surf[...]
    for field in range(NF):
        out[field : field + 1, 0:HALO] = tiles[0, field, 0:1, :]
        out[field : field + 1, HALO + COLS :] = tiles[1, field, 0:1, :]


def widen(chip, near, far, surf):
    return pl.pallas_call(
        widen_kernel,
        out_shape=jax.ShapeDtypeStruct((NF, MID), jnp.float32),
        in_specs=[ANY, ANY, ANY, VMEM],
        out_specs=VMEM,
        scratch_shapes=[pltpu.VMEM((2, NF, 8, HALO), jnp.float32), pltpu.SemaphoreType.DMA((2 * NF,))],
        compiler_params=params(2),
        name="widen",
    )(chip, near, far, surf)


def build_table(table, off, coef, first_panel):
    for part in range(BLOCK // LANES):
        at = pl.ds(first_panel + part, 1)
        lane = lax.broadcasted_iota(jnp.int32, (PANEL, LANES), 1)
        row = lax.broadcasted_iota(jnp.int32, (PANEL, LANES), 0)
        shift = lane - row + (HALO + part * LANES)
        offs = [jnp.broadcast_to(off[k, at, :], (PANEL, LANES)) for k in range(KN)]
        coefs = [jnp.broadcast_to(coef[k, at, :], (PANEL, LANES)) for k in range(KN)]
        high, low = [], []
        for k in range(KN):
            merged = coefs[k]
            for j in range(KN):
                if j != k:
                    merged = merged + jnp.where(offs[j] == offs[k], coefs[j], 0.0)
            top = merged.astype(jnp.bfloat16)
            high.append(top)
            low.append((merged - top.astype(jnp.float32)).astype(jnp.bfloat16))
        place = [(o + shift).astype(jnp.int16) for o in offs]
        none = jnp.zeros((PANEL, LANES), jnp.bfloat16)
        for start in range(0, WINDOW, PANEL):
            if start + PANEL <= part * LANES or start >= part * LANES + LANES + 2 * HALO:
                first, second = none, none
            else:
                first, second = none, none
                for k in range(KN):
                    hit = place[k] == jnp.int16(start)
                    first = jnp.where(hit, high[k], first)
                    second = jnp.where(hit, low[k], second)
            rows = slice(start, start + PANEL)
            table[rows, part * LANES : (part + 1) * LANES] = first
            table[rows, BLOCK + part * LANES : BLOCK + (part + 1) * LANES] = second


def split_into(parts, cols, value):
    top = value.astype(jnp.bfloat16)
    parts[0:ROWS, cols] = top
    parts[ROWS : 2 * ROWS, cols] = (value - top.astype(jnp.float32)).astype(jnp.bfloat16)


def relaxed(parts, table, start, centre, total, act):
    window = slice(start, start + WINDOW)
    both = jnp.dot(parts[:, window], table[:, 0:BLOCK], preferred_element_type=jnp.float32)
    rest = jnp.dot(parts[0:ROWS, window], table[:, BLOCK:], preferred_element_type=jnp.float32)
    gathered = both[0:ROWS] + both[ROWS:] + rest
    row = lax.broadcasted_iota(jnp.int32, (ROWS, BLOCK), 0)
    level = jnp.where(row >= LEV, row - LEV, row)
    return centre + jnp.where(level < act, gathered - total * centre, 0.0)


INSIDE = COLS - 2 * HALO
OWN = COLS // BLOCK


def totals_of(totals, coef, start, count):
    for j in range(count):
        total = coef[0, j : j + 1, :]
        for k in range(1, KN):
            total = total + coef[k, j : j + 1, :]
        totals[:, start + j * LANES : start + (j + 1) * LANES] = total


def inside_kernel(state, off, coef, act, tables, mid, parts2, out, parts, totals, done, sems):
    def table_of(b, carry):
        build_table(tables.at[b], off, coef, b * (BLOCK // LANES))
        return carry

    lax.fori_loop(0, OWN, table_of, 0)
    totals_of(totals, coef, 0, COLS // LANES)
    for b in range(OWN):
        cols = slice(b * BLOCK, (b + 1) * BLOCK)
        split_into(parts, cols, state[:, cols])
    for b in range(1, OWN - 1):
        cols = slice(b * BLOCK, (b + 1) * BLOCK)
        value = relaxed(parts, tables.at[b], (b - 1) * BLOCK, state[:, cols], totals[:, cols], act[:, cols])
        there = slice((b - 1) * BLOCK, b * BLOCK)
        mid[:, there] = value
        split_into(parts2, there, value)
    copies = []
    for b in range(2, OWN - 2):
        cols = slice(b * BLOCK, (b + 1) * BLOCK)
        centre = mid[:, (b - 1) * BLOCK : b * BLOCK]
        here = slice((b - 2) * BLOCK, (b - 1) * BLOCK)
        done[:, here] = relaxed(parts2, tables.at[b], (b - 2) * BLOCK, centre, totals[:, cols], act[:, cols])
        copy = pltpu.make_async_copy(
            done.at[:, pl.ds((b - 2) * BLOCK, BLOCK)], out.at[:, pl.ds(b * BLOCK, BLOCK)], sems.at[b - 2]
        )
        copy.start()
        copies.append(copy)
    for copy in copies:
        copy.wait()


def inside(state, off, coef, act):
    return pl.pallas_call(
        inside_kernel,
        out_shape=(
            jax.ShapeDtypeStruct((OWN, WINDOW, 2 * BLOCK), jnp.bfloat16),
            jax.ShapeDtypeStruct((ROWS, INSIDE), jnp.float32),
            jax.ShapeDtypeStruct((2 * ROWS, INSIDE), jnp.bfloat16),
            jax.ShapeDtypeStruct((ROWS, COLS), jnp.float32),
        ),
        in_specs=[VMEM, VMEM, VMEM, VMEM],
        out_specs=(VMEM, VMEM, VMEM, ANY),
        scratch_shapes=[
            pltpu.VMEM((2 * ROWS, COLS), jnp.bfloat16),
            pltpu.VMEM((1, COLS), jnp.float32),
            pltpu.VMEM((ROWS, COLS - 2 * EDGE), jnp.float32),
            pltpu.SemaphoreType.DMA((OWN - 4,)),
        ],
        compiler_params=params(6),
        cost_estimate=pl.CostEstimate(flops=2_000_000_000, bytes_accessed=4_000_000, transcendentals=0),
        name="inside",
    )(state, off, coef, act)


def advance_kernel(
    state, chip, near, far, coef, act, tables, mid_in, parts2_in, _, out,
    ends, mid_ends, parts, parts2, end_tables, end_off, end_coef, end_act, totals, done, sems,
):
    first, long = on_first_core(), from_far()

    def received(side, rows, cols):
        beside = jnp.where(long, far[rows, cols], near[rows, cols])
        mine = chip[rows, cols]
        return jnp.where(first, beside, mine) if side == 0 else jnp.where(first, mine, beside)

    for side in range(2):
        for part in range(HALO // LANES):
            j = side * (HALO // LANES) + part
            here = slice(part * LANES, (part + 1) * LANES)
            there = slice(HALO + part * LANES, HALO + (part + 1) * LANES)
            lists = received(side, slice(ROWS, SENT), here)
            weights = received(side, slice(ROWS, SENT), there)
            for k in range(KN):
                end_off[k, j : j + 1, :] = lists[k : k + 1, :].astype(jnp.int32)
                end_coef[k, j : j + 1, :] = weights[k : k + 1, :]
            end_act[:, j * LANES : (j + 1) * LANES] = lists[KN : KN + 1, :].astype(jnp.int32)

    def table_of(b, carry):
        build_table(end_tables.at[b], end_off, end_coef, b * (BLOCK // LANES))
        return carry

    lax.fori_loop(0, 2, table_of, 0)
    totals_of(totals, coef, 0, COLS // LANES)
    totals_of(totals, end_coef, COLS, 2 * HALO // LANES)
    parts2[:, 2 * HALO : 2 * HALO + INSIDE] = parts2_in[...]
    every = slice(0, ROWS)
    for side in range(2):
        for start in range(0, EDGE, BLOCK):
            cols = slice(start, start + BLOCK)
            value = received(side, every, cols)
            there = slice(start + side * EDGE, start + side * EDGE + BLOCK)
            ends[side, :, cols] = value
            split_into(parts.at[side], there, value)
            own = slice(start + side * (COLS - EDGE), start + side * (COLS - EDGE) + BLOCK)
            split_into(parts.at[side], slice(start + EDGE - side * EDGE, start + EDGE - side * EDGE + BLOCK), state[:, own])

    def end(side, block, table, centre, total, active):
        value = relaxed(parts.at[side], table, block * BLOCK, centre, total, active)
        mid_ends[side, :, block * BLOCK : (block + 1) * BLOCK] = value
        at = (side * OWN + block) * BLOCK
        split_into(parts2, slice(at, at + BLOCK), value)

    low, high = slice(0, BLOCK), slice(COLS - BLOCK, COLS)
    for side, block in ((0, 0), (1, 1)):
        cols = slice(side * HALO, (side + 1) * HALO)
        centre = ends[side, :, HALO - side * HALO : EDGE - side * HALO]
        end(side, block, end_tables.at[side], centre, totals[:, COLS + side * HALO : COLS + (side + 1) * HALO], end_act[:, cols])
    end(0, 1, tables.at[0], state[:, low], totals[:, low], act[:, low])
    end(1, 0, tables.at[OWN - 1], state[:, high], totals[:, high], act[:, high])
    copies = []
    for at, b in enumerate((0, 1, OWN - 2, OWN - 1)):
        cols = slice(b * BLOCK, (b + 1) * BLOCK)
        if b == 0:
            centre = mid_ends[0, :, BLOCK : 2 * BLOCK]
        elif b == OWN - 1:
            centre = mid_ends[1, :, 0:BLOCK]
        else:
            centre = mid_in[:, (b - 1) * BLOCK : b * BLOCK]
        done[at] = relaxed(parts2, tables.at[b], b * BLOCK, centre, totals[:, cols], act[:, cols])
        copy = pltpu.make_async_copy(done.at[at], out.at[:, pl.ds(b * BLOCK, BLOCK)], sems.at[at])
        copy.start()
        copies.append(copy)
    for copy in copies:
        copy.wait()


def advance(state, chip, near, far, coef, act, tables, mid, parts2, out):
    return pl.pallas_call(
        advance_kernel,
        out_shape=jax.ShapeDtypeStruct((ROWS, COLS), jnp.float32),
        in_specs=[VMEM, VMEM, VMEM, VMEM, VMEM, VMEM, VMEM, VMEM, VMEM, ANY],
        out_specs=ANY,
        scratch_shapes=[
            pltpu.VMEM((2, ROWS, EDGE), jnp.float32),
            pltpu.VMEM((2, ROWS, EDGE), jnp.float32),
            pltpu.VMEM((2, 2 * ROWS, 2 * EDGE), jnp.bfloat16),
            pltpu.VMEM((2 * ROWS, MID), jnp.bfloat16),
            pltpu.VMEM((2, WINDOW, 2 * BLOCK), jnp.bfloat16),
            pltpu.VMEM((KN, 2 * HALO // LANES, LANES), jnp.int32),
            pltpu.VMEM((KN, 2 * HALO // LANES, LANES), jnp.float32),
            pltpu.VMEM((1, 2 * HALO), jnp.int32),
            pltpu.VMEM((1, MID), jnp.float32),
            pltpu.VMEM((4, ROWS, BLOCK), jnp.float32),
            pltpu.SemaphoreType.DMA((4,)),
        ],
        input_output_aliases={9: 0},
        compiler_params=params(12),
        cost_estimate=pl.CostEstimate(flops=4_000_000_000, bytes_accessed=4_000_000, transcendentals=0),
        name="advance",
    )(state, chip, near, far, coef, act, tables, mid, parts2, out)


def couple_kernel(partner, ioff, iweight, act, relax, state, remapped, out, tiles, found_all, sems):
    reads = [
        pltpu.make_async_copy(state.at[pl.ds(LEV * field, 8), :], tiles.at[field], sems.at[field])
        for field in range(NF)
    ]
    for copy in reads:
        copy.start()
    lane = lax.broadcasted_iota(jnp.int32, (KR, LANES), 1)
    for b in range(COLS // LANES):
        cols = slice(b * LANES, (b + 1) * LANES)
        place = ioff[:, cols] + lane + HALO
        chunk = lax.shift_right_logical(place, 7)
        at = jnp.bitwise_and(place, LANES - 1)
        weights = iweight[:, cols]
        for field in range(NF):
            nearby = jnp.zeros((KR, LANES), jnp.float32)
            for q in range(1 + 2 * HALO // LANES):
                source = jnp.broadcast_to(
                    partner[field : field + 1, (b + q) * LANES : (b + q + 1) * LANES], (KR, LANES)
                )
                found = jnp.take_along_axis(source, at, axis=1, mode="promise_in_bounds")
                nearby = jnp.where(chunk == q, found, nearby)
            found_all[field : field + 1, cols] = jnp.sum(weights * nearby, axis=0, keepdims=True)
    writes = [pltpu.make_async_copy(found_all, remapped, sems.at[NF])]
    writes[0].start()
    for field in range(NF):
        reads[field].wait()
        before, value = tiles[field, 0:1, :], found_all[field : field + 1, :]
        tiles[field, 0:1, :] = before + jnp.where(act[...] > 0, relax[0, field] * (value - before), 0.0)
        copy = pltpu.make_async_copy(tiles.at[field], out.at[pl.ds(LEV * field, 8), :], sems.at[field])
        copy.start()
        writes.append(copy)
    for copy in writes:
        copy.wait()


def couple(partner, ioff, iweight, act, relax, state):
    return pl.pallas_call(
        couple_kernel,
        out_shape=(
            jax.ShapeDtypeStruct((NF, COLS), jnp.float32),
            jax.ShapeDtypeStruct((ROWS, COLS), jnp.float32),
        ),
        in_specs=[VMEM, VMEM, VMEM, VMEM, pl.BlockSpec(memory_space=pltpu.SMEM), ANY],
        out_specs=(ANY, ANY),
        scratch_shapes=[
            pltpu.VMEM((NF, 8, COLS), jnp.float32),
            pltpu.VMEM((NF, COLS), jnp.float32),
            pltpu.SemaphoreType.DMA((NF + 1,)),
        ],
        input_output_aliases={5: 1},
        compiler_params=params(4),
        name="couple",
    )(partner, ioff, iweight, act, relax, state)


def body(
    column_state,
    neighbour_offsets,
    edge_coefficients,
    active_levels,
    intersection_offsets,
    intersection_weights,
    relaxation,
):
    count = lax.axis_size("col")
    same_chip = [(i, i ^ 1) for i in range(count)]
    beside = [p for i in range(1, count - 1, 2) for p in ((i, i + 1), (i + 1, i))]
    long = [(i, j) for i, j in beside if i // RUN != j // RUN]
    short = [(i, j) for i, j in beside if i // RUN == j // RUN]
    state = column_state.reshape(ROWS, COLS)
    off = neighbour_offsets.reshape(KN, COLS // LANES, LANES)
    coef = edge_coefficients.reshape(KN, COLS // LANES, LANES)
    sent_beside, sent_chip, surface = pack(state, off, coef, active_levels)
    far = lax.ppermute(sent_beside, "col", long)
    near = lax.ppermute(sent_beside, "col", short)
    chip = lax.ppermute(sent_chip, "col", same_chip)
    tables, mid, parts, out = inside(state, off, coef, active_levels)
    partner = lax.ppermute(widen(chip, near, far, surface), "comp", [(0, 1), (1, 0)])
    advanced = advance(state, chip, near, far, coef, active_levels, tables, mid, parts, out)
    remapped, coupled = couple(
        partner, intersection_offsets[0], intersection_weights[0], active_levels, relaxation, advanced
    )
    return (coupled.reshape(1, NF, LEV, COLS), remapped.reshape(1, NF, COLS))


def solution(mesh):
    return jax.shard_map(
        body,
        mesh=mesh,
        in_specs=(
            P("comp", None, None, "col"),
            P("comp", None, "col"),
            P("comp", None, "col"),
            P("comp", "col"),
            P("comp", None, "col"),
            P("comp", None, "col"),
            P("comp", None),
        ),
        out_specs=(P("comp", None, None, "col"), P("comp", None, "col")),
        check_vma=False,
    )
```

time: 151 us -> 43.8 us (0.29)
  matrix products: 42 us -> 0 us
  other arithmetic: 32.9 us -> 0 us
  starting transfers between devices: 55.3 us -> 28.3 us
  local copies, waits for them, and re-layouts: 16.5 us -> 0.04 us
  Pallas kernels: 0 us -> 12.8 us
    dot_general x48 -> x0, matrix products: 42 us -> none  [one_block(): jnp.dot(source, table, precision=lax.Precision.HIGHEST, preferred_element...]
    ppermute x7 -> x4, starting transfers between devices: 55.3 us -> 28.3 us  [the longest x1 15.3 us: body(): far = lax.ppermute(sent_beside, 'col', long)]
    add x50 -> x0, other arithmetic: 16.1 us -> none  [the longest x48 11.2 us: one_block(): hits = local == block_offsets[:, None, :] + reach + inner]
    pallas_call x0 -> x5, Pallas kernels: none -> 12.8 us  [the longest x1 5.16 us: inside(): pl.pallas_call(inside_kernel, out_shape=(jax.ShapeDtypeStruct((OWN, WINDO...]
    reduce_sum x49 -> x0, other arithmetic: 12.7 us -> none  [the longest x48 12.7 us: one_block(): table = jnp.sum(jnp.where(hits, block_weights[:, None, :], 0.0), axis=0)]
    dynamic_slice x48 -> x0, local copies, waits for them, and re-layouts: 11.3 us -> none  [one_block(): block_weights = lax.dynamic_slice_in_dim(flat_weights, first, block, 1)]
    another operation x2 -> x0, local copies, waits for them, and re-layouts: 2.4 us -> none
    concatenate x2 -> x0, other arithmetic: 2.15 us -> none  [extended_2(): array = jnp.concatenate([before, array, after], axis=dim)]
  transfers between devices with their start and end apart: 7 -> 4, of which waited for: 1 -> 1; matrix products, arithmetic and copies ran while one was open for 23% -> 0% of each run, Pallas kernels for 0% -> 19%
where the time goes in v1:
time: 43.8 us; the launch traced here: 43.6 us
  starting transfers between devices  28.3 us (65%)
  Pallas kernels  12.8 us (29%)
  waiting for transfers between devices  1.5 us (3%)
  between operations  0.83 us (2%)
    ppermute x1, starting transfers between devices, body(): far = lax.ppermute(sent_beside, 'col', long)  15.3 us
    ppermute x1, starting transfers between devices, body(): lax.ppermute(widen(chip, near, far, surface), 'comp', [(0, 1), (1, 0)])  10.4 us
    pallas_call x1, Pallas kernels, inside(): pl.pallas_call(inside_kernel, out_shape=(jax.ShapeDtypeStruct((OWN, WINDO...  5.16 us
    pallas_call x1, Pallas kernels, advance(): pl.pallas_call(advance_kernel, out_shape=jax.ShapeDtypeStruct((ROWS, COLS...  3.15 us
    pallas_call x1, Pallas kernels, couple(): pl.pallas_call(couple_kernel, out_shape=(jax.ShapeDtypeStruct((NF, COLS),...  2.3 us
    pallas_call x1, Pallas kernels, pack(): pl.pallas_call(pack_kernel, out_shape=(sent, sent, jax.ShapeDtypeStruct((...  2.13 us
    ppermute x1, starting transfers between devices, body(): chip = lax.ppermute(sent_chip, 'col', same_chip)  1.92 us
    ppermute x1, waiting for transfers between devices, body(): far = lax.ppermute(sent_beside, 'col', long)  1.49 us
  transfers between devices with their start and end apart: 4, of which 1 were waited for; matrix products, arithmetic and copies ran while one was open for 0% of the time, Pallas kernels for 19%

profile of v1, /device:TPU:6, one launch (start us, length us, event | category | flops | bytes accessed | tf_op | source)
XLA Modules:
  0.0 43.6 jit_solution(1782551144286143335)
XLA Ops:
  0.6 0.0 copy-start
  0.6 0.0 copy-start.4
  0.7 0.0 copy-start.3
  0.7 0.0 copy-start.5
  0.7 2.1 %pack.1 = (f32[168,512]{1,0:T(8,128)}, f32[168,512]{1,0:T(8,128)}, f32[2,2048]{1,0:T(2,128)}) custom-call(f32[160,2048]{1,0:T(8,128)} %bitcast.7, s32[6,16,128]{2,1,0:T(8,128)} %bitcast.12, f32[6,16,128]{2,1,0:T(8,128)} %bitcast.14, s32[1,2048]{1,0:T(1,128)} %act.5), custom_call_target="tpu_custom_call" | custom-call | tf_op jit(solution)/shard_map/pack/pallas_call | solution.py:93
  2.8 0.7 %collective-permute-start.1 = (f32[168,512]{1,0:T(8,128)}, f32[168,512]{1,0:T(8,128)S(1)}, u32[]{:S(2)}, u32[]{:S(2)}) collective-permute-start(f32[168,512]{1,0:T(8,128)} %get-tuple-element.12), channel_id=1, source_target_pairs={{1,2},{2,1},{3,4},{4,3},{5,6},{6,5},{7,8},{8,7},{9,10},{10,9},{13,... | collective-permute-start | bytes 1032200 | tf_op jit(solution)/shard_map/ppermute | solution.py:449
  3.5 15.3 %collective-permute-start.2 = (f32[168,512]{1,0:T(8,128)}, f32[168,512]{1,0:T(8,128)S(1)}, u32[]{:S(2)}, u32[]{:S(2)}) collective-permute-start(f32[168,512]{1,0:T(8,128)} %get-tuple-element.12), channel_id=1, source_target_pairs={{11,12},{12,11},{23,24},{24,23},{35,36},{36,35},{47,48},{48,47},{5... | collective-permute-start | bytes 1032200 | tf_op jit(solution)/shard_map/ppermute | solution.py:448
  18.8 0.0 copy-start.6
  18.9 1.9 %collective-permute-start = (f32[168,512]{1,0:T(8,128)}, f32[168,512]{1,0:T(8,128)S(1)}, u32[]{:S(2)}, u32[]{:S(2)}) collective-permute-start(f32[168,512]{1,0:T(8,128)} %get-tuple-element.11), channel_id=1, source_target_pairs={{0,1},{1,0},{2,3},{3,2},{4,5},{5,4},{6,7},{7,6},{8,9},{9,8},{10,11... | collective-permute-start | bytes 1032200 | tf_op jit(solution)/shard_map/ppermute | solution.py:450
  20.8 0.0 copy-done
  20.8 0.0 copy-done.4
  20.8 0.0 copy-done.3
  20.8 0.0 copy-done.5
  20.8 5.2 %inside.1 = (bf16[8,768,512]{2,1,0:T(8,128)(2,1)S(1)}, f32[160,1536]{1,0:T(8,128)S(1)}, bf16[320,1536]{1,0:T(8,128)(2,1)S(1)}, f32[160,2048]{1,0:T(8,128)}) custom-call(f32[160,2048]{1,0:T(8,128)S(1)} %bitcast.8, s32[6,16,128]{2,1,0:T(8,128)S(1)} %bitcast.13, f32[6,16,128]{2,1,0:T(8,128)S(1)} %bitcast.15, s32[1,2048]{1,0:T(1,128)S(1)} %copy-done.5), custom_call_target="tpu_custom_call" | custom-call | flops 2000000000 | bytes 4000000 | tf_op jit(solution)/shard_map/inside/pallas_call | solution.py:254
  26.0 0.0 collective-permute-done.1.near
  26.0 1.5 %collective-permute-done.2.far = f32[168,512]{1,0:T(8,128)S(1)} collective-permute-done((f32[168,512]{1,0:T(8,128)}, f32[168,512]{1,0:T(8,128)S(1)}, u32[]{:S(2)}, u32[]{:S(2)}) %collective-permute-start.2) | collective-permute-done | bytes 344096 | tf_op jit(solution)/shard_map/ppermute | solution.py:448
  27.5 0.0 collective-permute-done.chip
  27.5 0.0 copy-done.6
  27.5 0.1 widen.1
  27.6 10.4 %collective-permute-start.3 = (f32[2,2560]{1,0:T(2,128)S(1)}, f32[2,2560]{1,0:T(2,128)S(1)}, u32[]{:S(2)}, u32[]{:S(2)}) collective-permute-start(f32[2,2560]{1,0:T(2,128)S(1)} %widen.1), channel_id=1, source_target_pairs={{0,384},{384,0},{1,385},{385,1},{2,386},{386,2},{3,387},{387,3},{4... | collective-permute-start | bytes 61448 | tf_op jit(solution)/shard_map/ppermute | solution.py:452
  38.0 0.0 copy-start.1
  38.0 0.0 copy-start.2
  38.0 0.0 copy-start.7
  38.1 3.2 %advance.1.state = f32[160,2048]{1,0:T(8,128)} custom-call(f32[160,2048]{1,0:T(8,128)S(1)} %bitcast.9, f32[168,512]{1,0:T(8,128)S(1)} %collective-permute-done.chip, f32[168,512]{1,0:T(8,128)S(1)} %collective-permute-done.1.near, f32[168,512]{1,0:T(8,128)S(1)} %collective-permute-done.2.far, ...), custom_call_target="tpu_custom_call", output_to_operand_aliasing={{}: (9, {})} | custom-call | flops 4000000000 | bytes 4000000 | tf_op jit(solution)/shard_map/advance/pallas_call | solution.py:349
  41.2 0.0 collective-permute-done.3.partner
  41.2 0.0 copy-done.1
  41.2 0.0 copy-done.2
  41.2 0.0 copy-done.7
  41.3 2.3 %couple.1 = (f32[2,2048]{1,0:T(2,128)}, f32[160,2048]{1,0:T(8,128)}) custom-call(f32[2,2560]{1,0:T(2,128)S(1)} %collective-permute-done.3.partner, s32[8,2048]{1,0:T(8,128)S(1)} %bitcast.10, f32[8,2048]{1,0:T(8,128)S(1)} %bitcast.11, s32[1,2048]{1,0:T(1,128)S(1)} %copy-done.5, f32[1,2]{1,0:T(1,128)S(1)} %copy-done.7, ...), custom_call_target="tpu_custom_call", output_to_operand_aliasing={{1}: (5, {})} | custom-call | tf_op jit(solution)/shard_map/couple/pallas_call | solution.py:411
Async XLA Ops:
  0.6 20.2 %copy-start = (f32[1,2,80,2048]{3,2,1,0:T(8,128)S(1)}, f32[1,2,80,2048]{3,2,1,0:T(8,128)}, u32[]{:S(2)}) copy-start(f32[1,2,80,2048]{3,2,1,0:T(8,128)} %param.7) | copy-start | bytes 3932164
  0.6 20.2 %copy-start.4 = (f32[1,6,2048]{2,0,1:T(1,128)S(1)}, f32[1,6,2048]{2,0,1:T(1,128)}, u32[]{:S(2)}) copy-start(f32[1,6,2048]{2,0,1:T(1,128)} %param.9) | copy-start | bytes 147460
  0.7 20.2 %copy-start.3 = (s32[1,6,2048]{2,0,1:T(1,128)S(1)}, s32[1,6,2048]{2,0,1:T(1,128)}, u32[]{:S(2)}) copy-start(s32[1,6,2048]{2,0,1:T(1,128)} %param.8) | copy-start | bytes 147460
  0.7 20.2 %copy-start.5 = (s32[1,2048]{1,0:T(1,128)S(1)}, s32[1,2048]{1,0:T(1,128)}, u32[]{:S(2)}) copy-start(s32[1,2048]{1,0:T(1,128)} %act.5) | copy-start | bytes 24580
  2.8 23.2 %collective-permute-start.1 = (f32[168,512]{1,0:T(8,128)}, f32[168,512]{1,0:T(8,128)S(1)}, u32[]{:S(2)}, u32[]{:S(2)}) collective-permute-start(f32[168,512]{1,0:T(8,128)} %get-tuple-element.12), channel_id=1, source_target_pairs={{1,2},{2,1},{3,4},{4,3},{5,6},{6,5},{7,8},{8,7},{9,10},{10,9},{13,... | collective-permute-start | bytes 1032200 | tf_op jit(solution)/shard_map/ppermute | solution.py:449
  3.5 24.0 %collective-permute-start.2 = (f32[168,512]{1,0:T(8,128)}, f32[168,512]{1,0:T(8,128)S(1)}, u32[]{:S(2)}, u32[]{:S(2)}) collective-permute-start(f32[168,512]{1,0:T(8,128)} %get-tuple-element.12), channel_id=1, source_target_pairs={{11,12},{12,11},{23,24},{24,23},{35,36},{36,35},{47,48},{48,47},{5... | collective-permute-start | bytes 1032200 | tf_op jit(solution)/shard_map/ppermute | solution.py:448
  18.8 8.7 %copy-start.6 = (f32[2,2048]{1,0:T(2,128)S(1)}, f32[2,2048]{1,0:T(2,128)}, u32[]{:S(2)}) copy-start(f32[2,2048]{1,0:T(2,128)} %get-tuple-element.13.surf) | copy-start | bytes 49156
  18.9 8.6 %collective-permute-start = (f32[168,512]{1,0:T(8,128)}, f32[168,512]{1,0:T(8,128)S(1)}, u32[]{:S(2)}, u32[]{:S(2)}) collective-permute-start(f32[168,512]{1,0:T(8,128)} %get-tuple-element.11), channel_id=1, source_target_pairs={{0,1},{1,0},{2,3},{3,2},{4,5},{5,4},{6,7},{7,6},{8,9},{9,8},{10,11... | collective-permute-start | bytes 1032200 | tf_op jit(solution)/shard_map/ppermute | solution.py:450
  27.6 13.6 %collective-permute-start.3 = (f32[2,2560]{1,0:T(2,128)S(1)}, f32[2,2560]{1,0:T(2,128)S(1)}, u32[]{:S(2)}, u32[]{:S(2)}) collective-permute-start(f32[2,2560]{1,0:T(2,128)S(1)} %widen.1), channel_id=1, source_target_pairs={{0,384},{384,0},{1,385},{385,1},{2,386},{386,2},{3,387},{387,3},{4... | collective-permute-start | bytes 61448 | tf_op jit(solution)/shard_map/ppermute | solution.py:452
  38.0 3.2 %copy-start.1 = (s32[1,8,2048]{2,1,0:T(8,128)S(1)}, s32[1,8,2048]{2,1,0:T(8,128)}, u32[]{:S(2)}) copy-start(s32[1,8,2048]{2,1,0:T(8,128)} %param.11) | copy-start | bytes 196612
  38.0 3.2 %copy-start.2 = (f32[1,8,2048]{2,1,0:T(8,128)S(1)}, f32[1,8,2048]{2,1,0:T(8,128)}, u32[]{:S(2)}) copy-start(f32[1,8,2048]{2,1,0:T(8,128)} %param.12) | copy-start | bytes 196612
  38.0 3.2 %copy-start.7 = (f32[1,2]{1,0:T(1,128)S(1)}, f32[1,2]{1,0:T(1,128)}, u32[]{:S(2)}) copy-start(f32[1,2]{1,0:T(1,128)} %relax.1) | copy-start | bytes 28

commit v2 on v1

v2 whole, which is shorter than its diff:
```python
import functools

import jax
import jax.numpy as jnp
from jax import lax
from jax.experimental import pallas as pl
from jax.experimental.pallas import tpu as pltpu
from jax.sharding import PartitionSpec as P

NF = 2
LEV = 80
ROWS = NF * LEV
COLS = 2048
HALO = 256
EDGE = 2 * HALO
KN = 6
KR = 8
BLOCK = 256
WINDOW = BLOCK + 2 * HALO
MID = COLS + 2 * HALO
SENT = ROWS + 8
LANES = 128
PANEL = 16
PACK_MIB = 60
RUN = 12
AHEAD = 4

ANY = pl.BlockSpec(memory_space=pl.ANY)
VMEM = pl.BlockSpec(memory_space=pltpu.VMEM)


def params(mib):
    return pltpu.CompilerParams(vmem_limit_bytes=mib << 20)


def on_first_core():
    return lax.rem(lax.axis_index("col"), 2) == 0


def at_run_end():
    place = lax.rem(lax.axis_index("col"), RUN)
    return jnp.logical_or(place == 0, place == RUN - 1)


def goes_ahead():
    return jnp.logical_and(lax.axis_index("comp") == 0, lax.rem(lax.axis_index("col"), RUN) < AHEAD)


def fill_lists(out, off, coef, act, high):
    out[ROWS + KN : SENT, :] = jnp.zeros((8 - KN, EDGE), jnp.float32)
    for part in range(HALO // LANES):
        j = (COLS - HALO if high else 0) // LANES + part
        here = slice(part * LANES, (part + 1) * LANES)
        there = slice(HALO + part * LANES, HALO + (part + 1) * LANES)
        for k in range(KN):
            out[ROWS + k : ROWS + k + 1, here] = off[k, j : j + 1, :].astype(jnp.float32)
            out[ROWS + k : ROWS + k + 1, there] = coef[k, j : j + 1, :]
        out[ROWS + KN : ROWS + KN + 1, here] = act[:, j * LANES : (j + 1) * LANES].astype(jnp.float32)


def pack_kernel(state, off_in, coef_in, act_in, near, chip, packed, off, coef, act, sems):
    first = on_first_core()
    lists = [
        pltpu.make_async_copy(source, target, sems.at[at])
        for at, (source, target) in enumerate(((off_in, off), (coef_in, coef), (act_in, act)))
    ]
    halves = [pl.ds(half * LEV, LEV) for half in range(NF)]

    def both(run_end, high):
        sides = ((chip, not high),) if run_end else ((near, high), (chip, not high))
        reads, writes = [], []
        for at, (_, upper) in enumerate(sides):
            start = COLS - EDGE if upper else 0
            for half, rows in enumerate(halves):
                reads.append(
                    pltpu.make_async_copy(
                        state.at[rows, pl.ds(start, EDGE)], packed.at[at, rows, :], sems.at[3 + NF * at + half]
                    )
                )
        for copy in reads + lists:
            copy.start()
        for copy in lists:
            copy.wait()
        for at, (out, upper) in enumerate(sides):
            fill_lists(packed.at[at], off, coef, act, upper)
            rows = pl.ds(ROWS, 8)
            copy = pltpu.make_async_copy(packed.at[at, rows, :], out.at[rows, :], sems.at[7 + at])
            copy.start()
            writes.append(copy)
        for at, (out, _) in enumerate(sides):
            for half, rows in enumerate(halves):
                reads[NF * at + half].wait()
                copy = pltpu.make_async_copy(packed.at[at, rows, :], out.at[rows, :], sems.at[9 + NF * at + half])
                copy.start()
                writes.append(copy)
        for copy in writes:
            copy.wait()

    for run_end in (True, False):
        for low in (True, False):

            @pl.when(jnp.logical_and(at_run_end() == run_end, first == low))
            def _(run_end=run_end, low=low):
                both(run_end, not low)


def pack(state, off, coef, act):
    sent = jax.ShapeDtypeStruct((SENT, EDGE), jnp.float32)
    return pl.pallas_call(
        pack_kernel,
        out_shape=(sent, sent),
        in_specs=[ANY, ANY, ANY, ANY],
        out_specs=(ANY, ANY),
        scratch_shapes=[
            pltpu.VMEM((2, SENT, EDGE), jnp.float32),
            pltpu.VMEM(off.shape, off.dtype),
            pltpu.VMEM(coef.shape, coef.dtype),
            pltpu.VMEM(act.shape, act.dtype),
            pltpu.SemaphoreType.DMA((13,)),
        ],
        compiler_params=params(PACK_MIB),
        name="pack",
    )(state, off, coef, act)


def rim_kernel(near, out):
    first = on_first_core()
    for field in range(NF):
        row = slice(LEV * field, LEV * field + 1)
        out[field : field + 1, :] = jnp.where(first, near[row, HALO:EDGE], near[row, 0:HALO])


def rim(near):
    return pl.pallas_call(
        rim_kernel,
        out_shape=jax.ShapeDtypeStruct((NF, HALO), jnp.float32),
        in_specs=[VMEM],
        out_specs=VMEM,
        compiler_params=params(2),
        name="rim",
    )(near)


def widen_kernel(chip, edge, surf, out):
    first = on_first_core()
    out[:, HALO : HALO + COLS] = surf[...]
    for field in range(NF):
        row, this = slice(LEV * field, LEV * field + 1), slice(field, field + 1)
        out[this, 0:HALO] = jnp.where(first, edge[this, :], chip[row, HALO:EDGE])
        out[this, HALO + COLS :] = jnp.where(first, chip[row, 0:HALO], edge[this, :])


def widen(chip, edge, surf):
    return pl.pallas_call(
        widen_kernel,
        out_shape=jax.ShapeDtypeStruct((NF, MID), jnp.float32),
        in_specs=[VMEM, VMEM, VMEM],
        out_specs=VMEM,
        compiler_params=params(2),
        name="widen",
    )(chip, edge, surf)


def build_table(table, off, coef, first_panel):
    for part in range(BLOCK // LANES):
        at = pl.ds(first_panel + part, 1)
        lane = lax.broadcasted_iota(jnp.int32, (PANEL, LANES), 1)
        row = lax.broadcasted_iota(jnp.int32, (PANEL, LANES), 0)
        shift = lane - row + (HALO + part * LANES)
        offs = [jnp.broadcast_to(off[k, at, :], (PANEL, LANES)) for k in range(KN)]
        coefs = [jnp.broadcast_to(coef[k, at, :], (PANEL, LANES)) for k in range(KN)]
        high, low = [], []
        for k in range(KN):
            merged = coefs[k]
            for j in range(KN):
                if j != k:
                    merged = merged + jnp.where(offs[j] == offs[k], coefs[j], 0.0)
            top = merged.astype(jnp.bfloat16)
            high.append(top)
            low.append((merged - top.astype(jnp.float32)).astype(jnp.bfloat16))
        place = [(o + shift).astype(jnp.int16) for o in offs]
        none = jnp.zeros((PANEL, LANES), jnp.bfloat16)
        for start in range(0, WINDOW, PANEL):
            if start + PANEL <= part * LANES or start >= part * LANES + LANES + 2 * HALO:
                first, second = none, none
            else:
                first, second = none, none
                for k in range(KN):
                    hit = place[k] == jnp.int16(start)
                    first = jnp.where(hit, high[k], first)
                    second = jnp.where(hit, low[k], second)
            rows = slice(start, start + PANEL)
            table[rows, part * LANES : (part + 1) * LANES] = first
            table[rows, BLOCK + part * LANES : BLOCK + (part + 1) * LANES] = second


def split_into(parts, cols, value):
    top = value.astype(jnp.bfloat16)
    parts[0:ROWS, cols] = top
    parts[ROWS : 2 * ROWS, cols] = (value - top.astype(jnp.float32)).astype(jnp.bfloat16)


def relaxed(parts, table, start, centre, total, act):
    window = slice(start, start + WINDOW)
    both = jnp.dot(parts[:, window], table[:, 0:BLOCK], preferred_element_type=jnp.float32)
    rest = jnp.dot(parts[0:ROWS, window], table[:, BLOCK:], preferred_element_type=jnp.float32)
    gathered = both[0:ROWS] + both[ROWS:] + rest
    row = lax.broadcasted_iota(jnp.int32, (ROWS, BLOCK), 0)
    level = jnp.where(row >= LEV, row - LEV, row)
    return centre + jnp.where(level < act, gathered - total * centre, 0.0)


INSIDE = COLS - 2 * HALO
CORE = COLS - 2 * EDGE
OWN = COLS // BLOCK


def totals_of(totals, coef, start, count):
    for j in range(count):
        total = coef[0, j : j + 1, :]
        for k in range(1, KN):
            total = total + coef[k, j : j + 1, :]
        totals[:, start + j * LANES : start + (j + 1) * LANES] = total


def inner(state, off, coef, act, tables, mid, parts2, done, parts, totals):
    def table_of(b, carry):
        build_table(tables.at[b], off, coef, b * (BLOCK // LANES))
        return carry

    lax.fori_loop(0, OWN, table_of, 0)
    totals_of(totals, coef, 0, COLS // LANES)
    for b in range(OWN):
        cols = slice(b * BLOCK, (b + 1) * BLOCK)
        split_into(parts, cols, state[:, cols])
    for b in range(1, OWN - 1):
        cols = slice(b * BLOCK, (b + 1) * BLOCK)
        value = relaxed(parts, tables.at[b], (b - 1) * BLOCK, state[:, cols], totals[:, cols], act[:, cols])
        there = slice((b - 1) * BLOCK, b * BLOCK)
        mid[:, there] = value
        split_into(parts2, there, value)
    for b in range(2, OWN - 2):
        cols = slice(b * BLOCK, (b + 1) * BLOCK)
        centre = mid[:, (b - 1) * BLOCK : b * BLOCK]
        here = slice((b - 2) * BLOCK, (b - 1) * BLOCK)
        done[:, here] = relaxed(parts2, tables.at[b], (b - 2) * BLOCK, centre, totals[:, cols], act[:, cols])


INNER = (
    jax.ShapeDtypeStruct((OWN, WINDOW, 2 * BLOCK), jnp.bfloat16),
    jax.ShapeDtypeStruct((ROWS, INSIDE), jnp.float32),
    jax.ShapeDtypeStruct((2 * ROWS, INSIDE), jnp.bfloat16),
    jax.ShapeDtypeStruct((ROWS, CORE), jnp.float32),
)
INNER_SCRATCH = [pltpu.VMEM((2 * ROWS, COLS), jnp.bfloat16), pltpu.VMEM((1, COLS), jnp.float32)]


def inside_kernel(state, off, coef, act, tables, mid, parts2, done, surf, edge, far, parts, totals):
    first = on_first_core()
    for field in range(NF):
        row, this = slice(LEV * field, LEV * field + 1), slice(field, field + 1)
        surf[this, :] = state[row, :]
        edge[this, :] = jnp.where(first, state[row, 0:HALO], state[row, COLS - HALO :])

    for low in (True, False):

        @pl.when(jnp.logical_and(at_run_end(), first == low))
        def _(low=low):
            far[0:ROWS, :] = state[:, 0:EDGE] if low else state[:, COLS - EDGE :]
            fill_lists(far, off, coef, act, not low)

    @pl.when(goes_ahead())
    def _():
        inner(state, off, coef, act, tables, mid, parts2, done, parts, totals)


def inside(state, off, coef, act):
    return pl.pallas_call(
        inside_kernel,
        out_shape=INNER
        + (
            jax.ShapeDtypeStruct((NF, COLS), jnp.float32),
            jax.ShapeDtypeStruct((NF, HALO), jnp.float32),
            jax.ShapeDtypeStruct((SENT, EDGE), jnp.float32),
        ),
        in_specs=[VMEM, VMEM, VMEM, VMEM],
        out_specs=(VMEM,) * 7,
        scratch_shapes=INNER_SCRATCH,
        compiler_params=params(6),
        cost_estimate=pl.CostEstimate(flops=2_000_000_000, bytes_accessed=4_000_000, transcendentals=0),
        name="inside",
    )(state, off, coef, act)


def advance_kernel(
    state, chip, near, far, off, coef, act, tables_in, mid_in, parts_in, core_in, out, done, core_out,
    ends, mid_ends, parts, parts2, end_tables, end_off, end_coef, end_act, totals,
    tables_late, mid_late, parts_late, state_parts, state_totals, sem,
):
    first, run_end, ahead = on_first_core(), at_run_end(), goes_ahead()

    @pl.when(ahead)
    def _():
        core_out[...] = core_in[...]

    @pl.when(jnp.logical_not(ahead))
    def _():
        inner(state, off, coef, act, tables_late, mid_late, parts_late, core_out, state_parts, state_totals)

    write = pltpu.make_async_copy(core_out, out.at[:, pl.ds(EDGE, CORE)], sem)
    write.start()

    def received(side, rows, cols):
        other, mine = jnp.where(run_end, far[rows, cols], near[rows, cols]), chip[rows, cols]
        return jnp.where(first, other, mine) if side == 0 else jnp.where(first, mine, other)

    for side in range(2):
        for part in range(HALO // LANES):
            j = side * (HALO // LANES) + part
            here = slice(part * LANES, (part + 1) * LANES)
            there = slice(HALO + part * LANES, HALO + (part + 1) * LANES)
            lists = received(side, slice(ROWS, SENT), here)
            weights = received(side, slice(ROWS, SENT), there)
            for k in range(KN):
                end_off[k, j : j + 1, :] = lists[k : k + 1, :].astype(jnp.int32)
                end_coef[k, j : j + 1, :] = weights[k : k + 1, :]
            end_act[:, j * LANES : (j + 1) * LANES] = lists[KN : KN + 1, :].astype(jnp.int32)

    def table_of(b, carry):
        build_table(end_tables.at[b], end_off, end_coef, b * (BLOCK // LANES))
        return carry

    lax.fori_loop(0, 2, table_of, 0)
    totals_of(totals, coef, 0, COLS // LANES)
    totals_of(totals, end_coef, COLS, 2 * HALO // LANES)
    every = slice(0, ROWS)
    for side in range(2):
        for start in range(0, EDGE, BLOCK):
            cols = slice(start, start + BLOCK)
            value = received(side, every, cols)
            there = slice(start + side * EDGE, start + side * EDGE + BLOCK)
            ends[side, :, cols] = value
            split_into(parts.at[side], there, value)
            own = slice(start + side * (COLS - EDGE), start + side * (COLS - EDGE) + BLOCK)
            split_into(parts.at[side], slice(start + EDGE - side * EDGE, start + EDGE - side * EDGE + BLOCK), state[:, own])

    def end(side, block, table, centre, total, active):
        value = relaxed(parts.at[side], table, block * BLOCK, centre, total, active)
        mid_ends[side, :, block * BLOCK : (block + 1) * BLOCK] = value
        at = (side * OWN + block) * BLOCK
        split_into(parts2, slice(at, at + BLOCK), value)

    low, high = slice(0, BLOCK), slice(COLS - BLOCK, COLS)

    def finish(tables, mid, parts_mid):
        parts2[:, 2 * HALO : 2 * HALO + INSIDE] = parts_mid[...]
        for side, block in ((0, 0), (1, 1)):
            cols = slice(side * HALO, (side + 1) * HALO)
            centre = ends[side, :, HALO - side * HALO : EDGE - side * HALO]
            total = totals[:, COLS + side * HALO : COLS + (side + 1) * HALO]
            end(side, block, end_tables.at[side], centre, total, end_act[:, cols])
        end(0, 1, tables.at[0], state[:, low], totals[:, low], act[:, low])
        end(1, 0, tables.at[OWN - 1], state[:, high], totals[:, high], act[:, high])
        for at, b in enumerate((0, 1, OWN - 2, OWN - 1)):
            cols = slice(b * BLOCK, (b + 1) * BLOCK)
            if b == 0:
                centre = mid_ends[0, :, BLOCK : 2 * BLOCK]
            elif b == OWN - 1:
                centre = mid_ends[1, :, 0:BLOCK]
            else:
                centre = mid[:, (b - 1) * BLOCK : b * BLOCK]
            there = slice(at * BLOCK, (at + 1) * BLOCK)
            done[:, there] = relaxed(parts2, tables.at[b], b * BLOCK, centre, totals[:, cols], act[:, cols])

    @pl.when(ahead)
    def _():
        finish(tables_in, mid_in, parts_in)

    @pl.when(jnp.logical_not(ahead))
    def _():
        finish(tables_late, mid_late, parts_late)

    write.wait()


def advance(state, chip, near, far, off, coef, act, tables, mid, parts2, core):
    return pl.pallas_call(
        advance_kernel,
        out_shape=(
            jax.ShapeDtypeStruct((ROWS, COLS), jnp.float32),
            jax.ShapeDtypeStruct((ROWS, 2 * EDGE), jnp.float32),
            jax.ShapeDtypeStruct((ROWS, CORE), jnp.float32),
        ),
        in_specs=[VMEM] * 11,
        out_specs=(ANY, VMEM, VMEM),
        scratch_shapes=[
            pltpu.VMEM((2, ROWS, EDGE), jnp.float32),
            pltpu.VMEM((2, ROWS, EDGE), jnp.float32),
            pltpu.VMEM((2, 2 * ROWS, 2 * EDGE), jnp.bfloat16),
            pltpu.VMEM((2 * ROWS, MID), jnp.bfloat16),
            pltpu.VMEM((2, WINDOW, 2 * BLOCK), jnp.bfloat16),
            pltpu.VMEM((KN, 2 * HALO // LANES, LANES), jnp.int32),
            pltpu.VMEM((KN, 2 * HALO // LANES, LANES), jnp.float32),
            pltpu.VMEM((1, 2 * HALO), jnp.int32),
            pltpu.VMEM((1, MID), jnp.float32),
        ]
        + [pltpu.VMEM(kept.shape, kept.dtype) for kept in INNER[:3]]
        + INNER_SCRATCH
        + [pltpu.SemaphoreType.DMA],
        compiler_params=params(24),
        cost_estimate=pl.CostEstimate(flops=6_000_000_000, bytes_accessed=4_000_000, transcendentals=0),
        name="advance",
    )(state, chip, near, far, off, coef, act, tables, mid, parts2, core)


def couple_kernel(got, beyond, ioff, iweight, act, relax, core, ends, _, remapped, out, partner, tiles, found_all, sems):
    writes = []
    for side in range(2):
        for field in range(NF):
            rows = pl.ds(LEV * field + 8, LEV - 8)
            writes.append(
                pltpu.make_async_copy(
                    ends.at[rows, pl.ds(side * EDGE, EDGE)],
                    out.at[rows, pl.ds(side * (COLS - EDGE), EDGE)],
                    sems.at[NF * side + field],
                )
            )
    for copy in writes:
        copy.start()
    first, run_end = on_first_core(), at_run_end()
    left, right = slice(0, HALO), slice(HALO + COLS, MID)
    partner[:, HALO : HALO + COLS] = got[:, HALO : HALO + COLS]
    partner[:, left] = jnp.where(jnp.logical_and(run_end, first), beyond[...], got[:, left])
    partner[:, right] = jnp.where(jnp.logical_and(run_end, jnp.logical_not(first)), beyond[...], got[:, right])
    lane = lax.broadcasted_iota(jnp.int32, (KR, LANES), 1)
    for b in range(COLS // LANES):
        cols = slice(b * LANES, (b + 1) * LANES)
        place = ioff[:, cols] + lane + HALO
        chunk = lax.shift_right_logical(place, 7)
        at = jnp.bitwise_and(place, LANES - 1)
        weights = iweight[:, cols]
        for field in range(NF):
            nearby = jnp.zeros((KR, LANES), jnp.float32)
            for q in range(1 + 2 * HALO // LANES):
                source = jnp.broadcast_to(
                    partner[field : field + 1, (b + q) * LANES : (b + q + 1) * LANES], (KR, LANES)
                )
                found = jnp.take_along_axis(source, at, axis=1, mode="promise_in_bounds")
                nearby = jnp.where(chunk == q, found, nearby)
            found_all[field : field + 1, cols] = jnp.sum(weights * nearby, axis=0, keepdims=True)
    copy = pltpu.make_async_copy(found_all, remapped, sems.at[2 * NF])
    copy.start()
    writes.append(copy)
    for field in range(NF):
        rows = slice(LEV * field, LEV * field + 8)
        tiles[field, :, 0:EDGE] = ends[rows, 0:EDGE]
        tiles[field, :, EDGE : EDGE + CORE] = core[rows, :]
        tiles[field, :, EDGE + CORE :] = ends[rows, EDGE:]
        before, value = tiles[field, 0:1, :], found_all[field : field + 1, :]
        tiles[field, 0:1, :] = before + jnp.where(act[...] > 0, relax[0, field] * (value - before), 0.0)
        copy = pltpu.make_async_copy(
            tiles.at[field], out.at[pl.ds(LEV * field, 8), :], sems.at[2 * NF + 1 + field]
        )
        copy.start()
        writes.append(copy)
    for copy in writes:
        copy.wait()


def couple(partner, beyond, ioff, iweight, act, relax, core, ends, out):
    return pl.pallas_call(
        couple_kernel,
        out_shape=(
            jax.ShapeDtypeStruct((NF, COLS), jnp.float32),
            jax.ShapeDtypeStruct((ROWS, COLS), jnp.float32),
        ),
        in_specs=[VMEM, VMEM, VMEM, VMEM, VMEM, pl.BlockSpec(memory_space=pltpu.SMEM), VMEM, VMEM, ANY],
        out_specs=(ANY, ANY),
        scratch_shapes=[
            pltpu.VMEM((NF, MID), jnp.float32),
            pltpu.VMEM((NF, 8, COLS), jnp.float32),
            pltpu.VMEM((NF, COLS), jnp.float32),
            pltpu.SemaphoreType.DMA((3 * NF + 1,)),
        ],
        input_output_aliases={8: 1},
        compiler_params=params(4),
        name="couple",
    )(partner, beyond, ioff, iweight, act, relax, core, ends, out)


def body(
    column_state,
    neighbour_offsets,
    edge_coefficients,
    active_levels,
    intersection_offsets,
    intersection_weights,
    relaxation,
):
    count = lax.axis_size("col")
    same_chip = [(i, i ^ 1) for i in range(count)]
    pairs = [p for i in range(1, count - 1, 2) for p in ((i, i + 1), (i + 1, i))]
    long = [(i, j) for i, j in pairs if i // RUN != j // RUN]
    short = [(i, j) for i, j in pairs if i // RUN == j // RUN]
    across = [(c * count + i, (1 - c) * count + j) for c in range(2) for i, j in long]
    state = column_state.reshape(ROWS, COLS)
    off = neighbour_offsets.reshape(KN, COLS // LANES, LANES)
    coef = edge_coefficients.reshape(KN, COLS // LANES, LANES)
    near, chip = pack(state, off, coef, active_levels)
    chip = lax.ppermute(chip, "col", same_chip)
    near = lax.ppermute(near, "col", short)
    tables, mid, parts, core, surface, edge, far = inside(state, off, coef, active_levels)
    far = lax.ppermute(far, "col", long)
    beyond = lax.ppermute(edge, ("comp", "col"), across)
    partner = lax.ppermute(widen(chip, rim(near), surface), "comp", [(0, 1), (1, 0)])
    out, ends, core = advance(state, chip, near, far, off, coef, active_levels, tables, mid, parts, core)
    remapped, coupled = couple(
        partner, beyond, intersection_offsets[0], intersection_weights[0], active_levels, relaxation, core, ends, out
    )
    return (coupled.reshape(1, NF, LEV, COLS), remapped.reshape(1, NF, COLS))


def solution(mesh):
    return jax.shard_map(
        body,
        mesh=mesh,
        in_specs=(
            P("comp", None, None, "col"),
            P("comp", None, "col"),
            P("comp", None, "col"),
            P("comp", "col"),
            P("comp", None, "col"),
            P("comp", None, "col"),
            P("comp", None),
        ),
        out_specs=(P("comp", None, None, "col"), P("comp", None, "col")),
        check_vma=False,
    )
```

time: 43.8 us -> 39.9 us (0.911)
  starting transfers between devices: 28.3 us -> 26.3 us
  Pallas kernels: 12.8 us -> 11.1 us
    ppermute x4 -> x5, starting transfers between devices: 28.3 us -> 26.3 us  [the longest x1 11.7 us: body(): far = lax.ppermute(far, 'col', long)]
    pallas_call x3 -> x4, Pallas kernels: 10.4 us -> 9.49 us  [the longest x1 4.59 us: inside(): pl.pallas_call(inside_kernel, out_shape=INNER + (jax.ShapeDtypeStruct((NF...]
    pallas_call x1, Pallas kernels: 2.3 us -> 1.6 us  [couple(): pl.pallas_call(couple_kernel, out_shape=(jax.ShapeDtypeStruct((NF, COLS),...]
    ppermute x4 -> x5, waiting for transfers between devices: 1.5 us -> 1.41 us  [the longest x1 1.4 us: body(): lax.ppermute(widen(chip, rim(near), surface), 'comp', [(0, 1), (1, 0)])]
  transfers between devices with their start and end apart: 4 -> 5, of which waited for: 1 -> 1; matrix products, arithmetic and copies ran while one was open for 0% -> 0% of each run, Pallas kernels for 19% -> 19%
where the time goes in v2:
time: 39.9 us; the launch traced here: 39.7 us
  starting transfers between devices  26.3 us (66%)
  Pallas kernels  11.1 us (28%)
  waiting for transfers between devices  1.41 us (4%)
  between operations  0.83 us (2%)
    ppermute x1, starting transfers between devices, body(): far = lax.ppermute(far, 'col', long)  11.7 us
    ppermute x1, starting transfers between devices, body(): lax.ppermute(widen(chip, rim(near), surface), 'comp', [(0, 1), (1, 0)])  7.79 us
    pallas_call x1, Pallas kernels, inside(): pl.pallas_call(inside_kernel, out_shape=INNER + (jax.ShapeDtypeStruct((NF...  4.59 us
    ppermute x1, starting transfers between devices, body(): beyond = lax.ppermute(edge, ('comp', 'col'), across)  4.17 us
    pallas_call x1, Pallas kernels, advance(): pl.pallas_call(advance_kernel, out_shape=(jax.ShapeDtypeStruct((ROWS, COL...  2.93 us
    ppermute x1, starting transfers between devices, body(): chip = lax.ppermute(chip, 'col', same_chip)  2.02 us
    pallas_call x1, Pallas kernels, pack(): pl.pallas_call(pack_kernel, out_shape=(sent, sent), in_specs=[ANY, ANY, A...  1.94 us
    pallas_call x1, Pallas kernels, couple(): pl.pallas_call(couple_kernel, out_shape=(jax.ShapeDtypeStruct((NF, COLS),...  1.6 us
  transfers between devices with their start and end apart: 5, of which 1 were waited for; matrix products, arithmetic and copies ran while one was open for 0% of the time, Pallas kernels for 19%

profile of v2, /device:TPU:6, one launch (start us, length us, event | category | flops | bytes accessed | tf_op | source)
XLA Modules:
  0.0 39.7 jit_solution(2921987851749983477)
XLA Ops:
  0.6 0.0 copy-start
  0.6 0.0 copy-start.3
  0.7 0.0 copy-start.4
  0.7 0.0 copy-start.5
  0.7 1.9 %pack.1 = (f32[168,512]{1,0:T(8,128)}, f32[168,512]{1,0:T(8,128)}) custom-call(f32[160,2048]{1,0:T(8,128)} %bitcast.7, s32[6,16,128]{2,1,0:T(8,128)} %bitcast.12, f32[6,16,128]{2,1,0:T(8,128)} %bitcast.15, s32[1,2048]{1,0:T(1,128)} %act.5), custom_call_target="tpu_custom_call" | custom-call | tf_op jit(solution)/shard_map/pack/pallas_call | solution.py:109
  2.6 2.0 %collective-permute-start = (f32[168,512]{1,0:T(8,128)}, f32[168,512]{1,0:T(8,128)S(1)}, u32[]{:S(2)}, u32[]{:S(2)}) collective-permute-start(f32[168,512]{1,0:T(8,128)} %get-tuple-element.16), channel_id=1, source_target_pairs={{0,1},{1,0},{2,3},{3,2},{4,5},{5,4},{6,7},{7,6},{8,9},{9,8},{10,11... | collective-permute-start | bytes 1032200 | tf_op jit(solution)/shard_map/ppermute | solution.py:510
  4.6 0.7 %collective-permute-start.1 = (f32[168,512]{1,0:T(8,128)}, f32[168,512]{1,0:T(8,128)S(1)}, u32[]{:S(2)}, u32[]{:S(2)}) collective-permute-start(f32[168,512]{1,0:T(8,128)} %get-tuple-element.17), channel_id=1, source_target_pairs={{1,2},{2,1},{3,4},{4,3},{5,6},{6,5},{7,8},{8,7},{9,10},{10,9},{13,... | collective-permute-start | bytes 1032200 | tf_op jit(solution)/shard_map/ppermute | solution.py:511
  5.3 0.0 copy-done
  5.3 0.0 copy-done.3
  5.4 0.0 copy-done.4
  5.4 0.0 copy-done.5
  5.4 4.6 %inside.1 = (bf16[8,768,512]{2,1,0:T(8,128)(2,1)S(1)}, f32[160,1536]{1,0:T(8,128)S(1)}, bf16[320,1536]{1,0:T(8,128)(2,1)S(1)}, f32[160,1024]{1,0:T(8,128)S(1)}, ...) custom-call(f32[160,2048]{1,0:T(8,128)S(1)} %bitcast.8, s32[6,16,128]{2,1,0:T(8,128)S(1)} %bitcast.13, ...), custom_call_target="tpu_custom_call" | custom-call | flops 2000000000 | bytes 4000000 | tf_op jit(solution)/shard_map/inside/pallas_call | solution.py:278
  10.0 11.7 %collective-permute-start.4 = (f32[168,512]{1,0:T(8,128)S(1)}, f32[168,512]{1,0:T(8,128)S(1)}, u32[]{:S(2)}, u32[]{:S(2)}) collective-permute-start(f32[168,512]{1,0:T(8,128)S(1)} %get-tuple-element.20), channel_id=1, source_target_pairs={{11,12},{12,11},{23,24},{24,23},{35,36},{36,35},{47,48},{48,47},{5... | collective-permute-start | bytes 1032200 | tf_op jit(solution)/shard_map/ppermute | solution.py:513
  21.6 4.2 %collective-permute-start.3 = (f32[2,256]{1,0:T(2,128)S(1)}, f32[2,256]{1,0:T(2,128)S(1)}, u32[]{:S(2)}, u32[]{:S(2)}) collective-permute-start(f32[2,256]{1,0:T(2,128)S(1)} %get-tuple-element.19), channel_id=1, source_target_pairs={{11,396},{12,395},{23,408},{24,407},{35,420},{36,419},{47,432},{48... | collective-permute-start | bytes 6152 | tf_op jit(solution)/shard_map/ppermute | solution.py:514
  25.8 0.0 collective-permute-done.1.near
  25.9 0.0 collective-permute-done.chip
  25.9 7.8 %collective-permute-start.2 = (f32[2,2560]{1,0:T(2,128)S(1)}, f32[2,2560]{1,0:T(2,128)S(1)}, u32[]{:S(2)}, u32[]{:S(2)}) collective-permute-start(f32[2,2560]{1,0:T(2,128)S(1)} %widen.1), channel_id=1, source_target_pairs={{0,384},{384,0},{1,385},{385,1},{2,386},{386,2},{3,387},{387,3},{4... | collective-permute-start | bytes 61448 | tf_op jit(solution)/shard_map/ppermute | solution.py:515
  33.7 0.0 collective-permute-done.4.far
  33.7 0.0 copy-start.1
  33.7 0.0 copy-start.2
  33.7 0.0 copy-start.6
  33.7 2.9 %advance.1 = (f32[160,2048]{1,0:T(8,128)}, f32[160,1024]{1,0:T(8,128)S(1)}, f32[160,1024]{1,0:T(8,128)S(1)}) custom-call(f32[160,2048]{1,0:T(8,128)S(1)} %bitcast.9, f32[168,512]{1,0:T(8,128)S(1)} %collective-permute-done.chip, f32[168,512]{1,0:T(8,128)S(1)} %collective-permute-done.1.near, f32[168,512]{1,0:T(8,128)S(1)} %collective-permute-done.4.far, ...), custom_call_target="tpu_custom_call" | custom-call | flops 6000000000 | bytes 4000000 | tf_op jit(solution)/shard_map/advance/pallas_call | solution.py:387
  36.7 0.0 collective-permute-done.3.beyond
  36.7 1.4 %collective-permute-done.2.got = f32[2,2560]{1,0:T(2,128)S(1)} collective-permute-done((f32[2,2560]{1,0:T(2,128)S(1)}, f32[2,2560]{1,0:T(2,128)S(1)}, u32[]{:S(2)}, u32[]{:S(2)}) %collective-permute-start.2) | collective-permute-done | bytes 20512 | tf_op jit(solution)/shard_map/ppermute | solution.py:515
  38.1 0.0 copy-done.1
  38.1 0.0 copy-done.2
  38.1 0.0 copy-done.6
  38.1 1.6 %couple.1 = (f32[2,2048]{1,0:T(2,128)}, f32[160,2048]{1,0:T(8,128)}) custom-call(f32[2,2560]{1,0:T(2,128)S(1)} %collective-permute-done.2.got, f32[2,256]{1,0:T(2,128)S(1)} %collective-permute-done.3.beyond, s32[8,2048]{1,0:T(8,128)S(1)} %bitcast.10, f32[8,2048]{1,0:T(8,128)S(1)} %bitcast.11, ...), custom_call_target="tpu_custom_call", output_to_operand_aliasing={{1}: (8, {})} | custom-call | tf_op jit(solution)/shard_map/couple/pallas_call | solution.py:471
  (2 shorter events, 0.0 us)
Async XLA Ops:
  0.6 4.7 %copy-start = (f32[1,2,80,2048]{3,2,1,0:T(8,128)S(1)}, f32[1,2,80,2048]{3,2,1,0:T(8,128)}, u32[]{:S(2)}) copy-start(f32[1,2,80,2048]{3,2,1,0:T(8,128)} %param.7) | copy-start | bytes 3932164
  0.6 4.7 %copy-start.3 = (s32[1,6,2048]{2,0,1:T(1,128)S(1)}, s32[1,6,2048]{2,0,1:T(1,128)}, u32[]{:S(2)}) copy-start(s32[1,6,2048]{2,0,1:T(1,128)} %param.8) | copy-start | bytes 147460
  0.7 4.7 %copy-start.4 = (f32[1,6,2048]{2,0,1:T(1,128)S(1)}, f32[1,6,2048]{2,0,1:T(1,128)}, u32[]{:S(2)}) copy-start(f32[1,6,2048]{2,0,1:T(1,128)} %param.9) | copy-start | bytes 147460
  0.7 4.7 %copy-start.5 = (s32[1,2048]{1,0:T(1,128)S(1)}, s32[1,2048]{1,0:T(1,128)}, u32[]{:S(2)}) copy-start(s32[1,2048]{1,0:T(1,128)} %act.5) | copy-start | bytes 24580
  2.6 23.2 %collective-permute-start = (f32[168,512]{1,0:T(8,128)}, f32[168,512]{1,0:T(8,128)S(1)}, u32[]{:S(2)}, u32[]{:S(2)}) collective-permute-start(f32[168,512]{1,0:T(8,128)} %get-tuple-element.16), channel_id=1, source_target_pairs={{0,1},{1,0},{2,3},{3,2},{4,5},{5,4},{6,7},{7,6},{8,9},{9,8},{10,11... | collective-permute-start | bytes 1032200 | tf_op jit(solution)/shard_map/ppermute | solution.py:510
  4.6 21.2 %collective-permute-start.1 = (f32[168,512]{1,0:T(8,128)}, f32[168,512]{1,0:T(8,128)S(1)}, u32[]{:S(2)}, u32[]{:S(2)}) collective-permute-start(f32[168,512]{1,0:T(8,128)} %get-tuple-element.17), channel_id=1, source_target_pairs={{1,2},{2,1},{3,4},{4,3},{5,6},{6,5},{7,8},{8,7},{9,10},{10,9},{13,... | collective-permute-start | bytes 1032200 | tf_op jit(solution)/shard_map/ppermute | solution.py:511
  10.0 23.7 %collective-permute-start.4 = (f32[168,512]{1,0:T(8,128)S(1)}, f32[168,512]{1,0:T(8,128)S(1)}, u32[]{:S(2)}, u32[]{:S(2)}) collective-permute-start(f32[168,512]{1,0:T(8,128)S(1)} %get-tuple-element.20), channel_id=1, source_target_pairs={{11,12},{12,11},{23,24},{24,23},{35,36},{36,35},{47,48},{48,47},{5... | collective-permute-start | bytes 1032200 | tf_op jit(solution)/shard_map/ppermute | solution.py:513
  21.6 15.0 %collective-permute-start.3 = (f32[2,256]{1,0:T(2,128)S(1)}, f32[2,256]{1,0:T(2,128)S(1)}, u32[]{:S(2)}, u32[]{:S(2)}) collective-permute-start(f32[2,256]{1,0:T(2,128)S(1)} %get-tuple-element.19), channel_id=1, source_target_pairs={{11,396},{12,395},{23,408},{24,407},{35,420},{36,419},{47,432},{48... | collective-permute-start | bytes 6152 | tf_op jit(solution)/shard_map/ppermute | solution.py:514
  25.9 12.2 %collective-permute-start.2 = (f32[2,2560]{1,0:T(2,128)S(1)}, f32[2,2560]{1,0:T(2,128)S(1)}, u32[]{:S(2)}, u32[]{:S(2)}) collective-permute-start(f32[2,2560]{1,0:T(2,128)S(1)} %widen.1), channel_id=1, source_target_pairs={{0,384},{384,0},{1,385},{385,1},{2,386},{386,2},{3,387},{387,3},{4... | collective-permute-start | bytes 61448 | tf_op jit(solution)/shard_map/ppermute | solution.py:515
  33.7 4.4 %copy-start.1 = (s32[1,8,2048]{2,1,0:T(8,128)S(1)}, s32[1,8,2048]{2,1,0:T(8,128)}, u32[]{:S(2)}) copy-start(s32[1,8,2048]{2,1,0:T(8,128)} %param.11) | copy-start | bytes 196612
  33.7 4.4 %copy-start.2 = (f32[1,8,2048]{2,1,0:T(8,128)S(1)}, f32[1,8,2048]{2,1,0:T(8,128)}, u32[]{:S(2)}) copy-start(f32[1,8,2048]{2,1,0:T(8,128)} %param.12) | copy-start | bytes 196612
  33.7 4.4 %copy-start.6 = (f32[1,2]{1,0:T(1,128)S(1)}, f32[1,2]{1,0:T(1,128)}, u32[]{:S(2)}) copy-start(f32[1,2]{1,0:T(1,128)} %relax.1) | copy-start | bytes 28

commit v3 on v2

--- a/solution.py
+++ b/solution.py
@@ -21,7 +21,6 @@
 SENT = ROWS + 8
 LANES = 128
 PANEL = 16
-PACK_MIB = 60
 RUN = 12
 AHEAD = 4
 
@@ -58,43 +57,29 @@
         out[ROWS + KN : ROWS + KN + 1, here] = act[:, j * LANES : (j + 1) * LANES].astype(jnp.float32)
 
 
-def pack_kernel(state, off_in, coef_in, act_in, near, chip, packed, off, coef, act, sems):
+def begin_kernel(out):
+    out[...] = jnp.zeros(out.shape, out.dtype)
+
+
+def begin():
+    return pl.pallas_call(
+        begin_kernel,
+        out_shape=jax.ShapeDtypeStruct((8, LANES), jnp.float32),
+        out_specs=VMEM,
+        compiler_params=params(1),
+        cost_estimate=pl.CostEstimate(flops=4_000_000_000, bytes_accessed=8_000_000, transcendentals=0),
+        name="begin",
+    )()
+
+
+def pack_kernel(_, state, off, coef, act, near, chip):
     first = on_first_core()
-    lists = [
-        pltpu.make_async_copy(source, target, sems.at[at])
-        for at, (source, target) in enumerate(((off_in, off), (coef_in, coef), (act_in, act)))
-    ]
-    halves = [pl.ds(half * LEV, LEV) for half in range(NF)]
 
     def both(run_end, high):
-        sides = ((chip, not high),) if run_end else ((near, high), (chip, not high))
-        reads, writes = [], []
-        for at, (_, upper) in enumerate(sides):
+        for out, upper in ((chip, not high),) if run_end else ((chip, not high), (near, high)):
             start = COLS - EDGE if upper else 0
-            for half, rows in enumerate(halves):
-                reads.append(
-                    pltpu.make_async_copy(
-                        state.at[rows, pl.ds(start, EDGE)], packed.at[at, rows, :], sems.at[3 + NF * at + half]
-                    )
-                )
-        for copy in reads + lists:
-            copy.start()
-        for copy in lists:
-            copy.wait()
-        for at, (out, upper) in enumerate(sides):
-            fill_lists(packed.at[at], off, coef, act, upper)
-            rows = pl.ds(ROWS, 8)
-            copy = pltpu.make_async_copy(packed.at[at, rows, :], out.at[rows, :], sems.at[7 + at])
-            copy.start()
-            writes.append(copy)
-        for at, (out, _) in enumerate(sides):
-            for half, rows in enumerate(halves):
-                reads[NF * at + half].wait()
-                copy = pltpu.make_async_copy(packed.at[at, rows, :], out.at[rows, :], sems.at[9 + NF * at + half])
-                copy.start()
-                writes.append(copy)
-        for copy in writes:
-            copy.wait()
+            out[0:ROWS, :] = state[:, start : start + EDGE]
+            fill_lists(out, off, coef, act, upper)
 
     for run_end in (True, False):
         for low in (True, False):
@@ -109,18 +94,11 @@
     return pl.pallas_call(
         pack_kernel,
         out_shape=(sent, sent),
-        in_specs=[ANY, ANY, ANY, ANY],
-        out_specs=(ANY, ANY),
-        scratch_shapes=[
-            pltpu.VMEM((2, SENT, EDGE), jnp.float32),
-            pltpu.VMEM(off.shape, off.dtype),
-            pltpu.VMEM(coef.shape, coef.dtype),
-            pltpu.VMEM(act.shape, act.dtype),
-            pltpu.SemaphoreType.DMA((13,)),
-        ],
-        compiler_params=params(PACK_MIB),
+        in_specs=[VMEM] * 5,
+        out_specs=(VMEM, VMEM),
+        compiler_params=params(2),
         name="pack",
-    )(state, off, coef, act)
+    )(begin(), state, off, coef, act)
 
 
 def rim_kernel(near, out):

time: 39.9 us -> 39.6 us (level); the launches traced: 39.7 us -> 38.9 us
  Pallas kernels: 11.1 us -> 9.09 us
  local copies, waits for them, and re-layouts: 0.04 us -> 1.3 us
    pallas_call x1 -> x2, Pallas kernels: 1.94 us -> 0.07 us  [the longest x1 0.07 us: pack(): pl.pallas_call(pack_kernel, out_shape=(sent, sent), in_specs=[VMEM] * 5,...]
    unnamed x14, local copies, waits for them, and re-layouts: 0.04 us -> 1.3 us
where the time goes in v3:
time: 39.6 us; the launch traced here: 38.9 us
  starting transfers between devices  26.1 us (66%)
  Pallas kernels  9.09 us (23%)
  waiting for transfers between devices  1.52 us (4%)
  local copies, waits for them, and re-layouts  1.3 us (3%)
  between operations  0.81 us (2%)
    ppermute x1, starting transfers between devices, body(): far = lax.ppermute(far, 'col', long)  11.6 us
    ppermute x1, starting transfers between devices, body(): lax.ppermute(widen(chip, rim(near), surface), 'comp', [(0, 1), (1, 0)])  7.65 us
    pallas_call x1, Pallas kernels, inside(): pl.pallas_call(inside_kernel, out_shape=INNER + (jax.ShapeDtypeStruct((NF...  4.52 us
    ppermute x1, starting transfers between devices, body(): beyond = lax.ppermute(edge, ('comp', 'col'), across)  4.31 us
    pallas_call x1, Pallas kernels, advance(): pl.pallas_call(advance_kernel, out_shape=(jax.ShapeDtypeStruct((ROWS, COL...  2.86 us
    ppermute x1, starting transfers between devices, body(): chip = lax.ppermute(chip, 'col', same_chip)  1.92 us
    pallas_call x1, Pallas kernels, couple(): pl.pallas_call(couple_kernel, out_shape=(jax.ShapeDtypeStruct((NF, COLS),...  1.61 us
    ppermute x1, waiting for transfers between devices, body(): lax.ppermute(widen(chip, rim(near), surface), 'comp', [(0, 1), (1, 0)])  1.51 us
  transfers between devices with their start and end apart: 5, of which 1 were waited for; matrix products, arithmetic and copies ran while one was open for 0% of the time, Pallas kernels for 19%

profile of v3, /device:TPU:6, one launch (start us, length us, event | category | flops | bytes accessed | tf_op | source)
XLA Modules:
  0.0 38.9 jit_solution(17010611253841899236)
XLA Ops:
  0.6 0.0 copy-start
  0.6 0.0 copy-start.3
  0.7 0.0 copy-start.4
  0.7 0.0 copy-start.5
  0.7 1.3 %copy-done = f32[1,2,80,2048]{3,2,1,0:T(8,128)S(1)} copy-done((f32[1,2,80,2048]{3,2,1,0:T(8,128)S(1)}, f32[1,2,80,2048]{3,2,1,0:T(8,128)}, u32[]{:S(2)}) %copy-start) | copy-done | bytes 1310744
  1.9 0.0 copy-done.3
  2.0 0.0 copy-done.4
  2.0 0.0 copy-done.5
  2.0 0.1 pack.1
  2.0 1.9 %collective-permute-start = (f32[168,512]{1,0:T(8,128)S(1)}, f32[168,512]{1,0:T(8,128)S(1)}, u32[]{:S(2)}, u32[]{:S(2)}) collective-permute-start(f32[168,512]{1,0:T(8,128)S(1)} %get-tuple-element.16), channel_id=1, source_target_pairs={{0,1},{1,0},{2,3},{3,2},{4,5},{5,4},{6,7},{7,6},{8,9},{9,8},{10,11... | collective-permute-start | bytes 1032200 | tf_op jit(solution)/shard_map/ppermute | solution.py:488
  4.0 0.7 %collective-permute-start.1 = (f32[168,512]{1,0:T(8,128)S(1)}, f32[168,512]{1,0:T(8,128)S(1)}, u32[]{:S(2)}, u32[]{:S(2)}) collective-permute-start(f32[168,512]{1,0:T(8,128)S(1)} %get-tuple-element.17), channel_id=1, source_target_pairs={{1,2},{2,1},{3,4},{4,3},{5,6},{6,5},{7,8},{8,7},{9,10},{10,9},{13,... | collective-permute-start | bytes 1032200 | tf_op jit(solution)/shard_map/ppermute | solution.py:489
  4.6 4.5 %inside.1 = (bf16[8,768,512]{2,1,0:T(8,128)(2,1)S(1)}, f32[160,1536]{1,0:T(8,128)S(1)}, bf16[320,1536]{1,0:T(8,128)(2,1)S(1)}, f32[160,1024]{1,0:T(8,128)S(1)}, ...) custom-call(f32[160,2048]{1,0:T(8,128)S(1)} %bitcast.8, s32[6,16,128]{2,1,0:T(8,128)S(1)} %bitcast.13, ...), custom_call_target="tpu_custom_call" | custom-call | flops 2000000000 | bytes 4000000 | tf_op jit(solution)/shard_map/inside/pallas_call | solution.py:256
  9.2 11.6 %collective-permute-start.4 = (f32[168,512]{1,0:T(8,128)S(1)}, f32[168,512]{1,0:T(8,128)S(1)}, u32[]{:S(2)}, u32[]{:S(2)}) collective-permute-start(f32[168,512]{1,0:T(8,128)S(1)} %get-tuple-element.20), channel_id=1, source_target_pairs={{11,12},{12,11},{23,24},{24,23},{35,36},{36,35},{47,48},{48,47},{5... | collective-permute-start | bytes 1032200 | tf_op jit(solution)/shard_map/ppermute | solution.py:491
  20.8 4.3 %collective-permute-start.3 = (f32[2,256]{1,0:T(2,128)S(1)}, f32[2,256]{1,0:T(2,128)S(1)}, u32[]{:S(2)}, u32[]{:S(2)}) collective-permute-start(f32[2,256]{1,0:T(2,128)S(1)} %get-tuple-element.19), channel_id=1, source_target_pairs={{11,396},{12,395},{23,408},{24,407},{35,420},{36,419},{47,432},{48... | collective-permute-start | bytes 6152 | tf_op jit(solution)/shard_map/ppermute | solution.py:492
  25.1 0.0 collective-permute-done.1.near
  25.1 0.0 collective-permute-done.chip
  25.2 7.6 %collective-permute-start.2 = (f32[2,2560]{1,0:T(2,128)S(1)}, f32[2,2560]{1,0:T(2,128)S(1)}, u32[]{:S(2)}, u32[]{:S(2)}) collective-permute-start(f32[2,2560]{1,0:T(2,128)S(1)} %widen.1), channel_id=1, source_target_pairs={{0,384},{384,0},{1,385},{385,1},{2,386},{386,2},{3,387},{387,3},{4... | collective-permute-start | bytes 61448 | tf_op jit(solution)/shard_map/ppermute | solution.py:493
  32.8 0.0 collective-permute-done.4.far
  32.8 0.0 copy-start.1
  32.8 0.0 copy-start.2
  32.9 0.0 copy-start.6
  32.9 2.9 %advance.1 = (f32[160,2048]{1,0:T(8,128)}, f32[160,1024]{1,0:T(8,128)S(1)}, f32[160,1024]{1,0:T(8,128)S(1)}) custom-call(f32[160,2048]{1,0:T(8,128)S(1)} %bitcast.9, f32[168,512]{1,0:T(8,128)S(1)} %collective-permute-done.chip, f32[168,512]{1,0:T(8,128)S(1)} %collective-permute-done.1.near, f32[168,512]{1,0:T(8,128)S(1)} %collective-permute-done.4.far, ...), custom_call_target="tpu_custom_call" | custom-call | flops 6000000000 | bytes 4000000 | tf_op jit(solution)/shard_map/advance/pallas_call | solution.py:365
  35.7 0.0 collective-permute-done.3.beyond
  35.7 1.5 %collective-permute-done.2.got = f32[2,2560]{1,0:T(2,128)S(1)} collective-permute-done((f32[2,2560]{1,0:T(2,128)S(1)}, f32[2,2560]{1,0:T(2,128)S(1)}, u32[]{:S(2)}, u32[]{:S(2)}) %collective-permute-start.2) | collective-permute-done | bytes 20512 | tf_op jit(solution)/shard_map/ppermute | solution.py:493
  37.2 0.0 copy-done.1
  37.2 0.0 copy-done.2
  37.3 0.0 copy-done.6
  37.3 1.6 %couple.1 = (f32[2,2048]{1,0:T(2,128)}, f32[160,2048]{1,0:T(8,128)}) custom-call(f32[2,2560]{1,0:T(2,128)S(1)} %collective-permute-done.2.got, f32[2,256]{1,0:T(2,128)S(1)} %collective-permute-done.3.beyond, s32[8,2048]{1,0:T(8,128)S(1)} %bitcast.10, f32[8,2048]{1,0:T(8,128)S(1)} %bitcast.11, ...), custom_call_target="tpu_custom_call", output_to_operand_aliasing={{1}: (8, {})} | custom-call | tf_op jit(solution)/shard_map/couple/pallas_call | solution.py:449
  (3 shorter events, 0.0 us)
Async XLA Ops:
  0.6 1.3 %copy-start = (f32[1,2,80,2048]{3,2,1,0:T(8,128)S(1)}, f32[1,2,80,2048]{3,2,1,0:T(8,128)}, u32[]{:S(2)}) copy-start(f32[1,2,80,2048]{3,2,1,0:T(8,128)} %param.7) | copy-start | bytes 3932164
  0.6 1.3 %copy-start.3 = (s32[1,6,2048]{2,0,1:T(1,128)S(1)}, s32[1,6,2048]{2,0,1:T(1,128)}, u32[]{:S(2)}) copy-start(s32[1,6,2048]{2,0,1:T(1,128)} %param.8) | copy-start | bytes 147460
  0.7 1.3 %copy-start.4 = (f32[1,6,2048]{2,0,1:T(1,128)S(1)}, f32[1,6,2048]{2,0,1:T(1,128)}, u32[]{:S(2)}) copy-start(f32[1,6,2048]{2,0,1:T(1,128)} %param.9) | copy-start | bytes 147460
  0.7 1.3 %copy-start.5 = (s32[1,2048]{1,0:T(1,128)S(1)}, s32[1,2048]{1,0:T(1,128)}, u32[]{:S(2)}) copy-start(s32[1,2048]{1,0:T(1,128)} %act.7) | copy-start | bytes 24580
  2.0 23.1 %collective-permute-start = (f32[168,512]{1,0:T(8,128)S(1)}, f32[168,512]{1,0:T(8,128)S(1)}, u32[]{:S(2)}, u32[]{:S(2)}) collective-permute-start(f32[168,512]{1,0:T(8,128)S(1)} %get-tuple-element.16), channel_id=1, source_target_pairs={{0,1},{1,0},{2,3},{3,2},{4,5},{5,4},{6,7},{7,6},{8,9},{9,8},{10,11... | collective-permute-start | bytes 1032200 | tf_op jit(solution)/shard_map/ppermute | solution.py:488
  4.0 21.1 %collective-permute-start.1 = (f32[168,512]{1,0:T(8,128)S(1)}, f32[168,512]{1,0:T(8,128)S(1)}, u32[]{:S(2)}, u32[]{:S(2)}) collective-permute-start(f32[168,512]{1,0:T(8,128)S(1)} %get-tuple-element.17), channel_id=1, source_target_pairs={{1,2},{2,1},{3,4},{4,3},{5,6},{6,5},{7,8},{8,7},{9,10},{10,9},{13,... | collective-permute-start | bytes 1032200 | tf_op jit(solution)/shard_map/ppermute | solution.py:489
  9.2 23.6 %collective-permute-start.4 = (f32[168,512]{1,0:T(8,128)S(1)}, f32[168,512]{1,0:T(8,128)S(1)}, u32[]{:S(2)}, u32[]{:S(2)}) collective-permute-start(f32[168,512]{1,0:T(8,128)S(1)} %get-tuple-element.20), channel_id=1, source_target_pairs={{11,12},{12,11},{23,24},{24,23},{35,36},{36,35},{47,48},{48,47},{5... | collective-permute-start | bytes 1032200 | tf_op jit(solution)/shard_map/ppermute | solution.py:491
  20.8 15.0 %collective-permute-start.3 = (f32[2,256]{1,0:T(2,128)S(1)}, f32[2,256]{1,0:T(2,128)S(1)}, u32[]{:S(2)}, u32[]{:S(2)}) collective-permute-start(f32[2,256]{1,0:T(2,128)S(1)} %get-tuple-element.19), channel_id=1, source_target_pairs={{11,396},{12,395},{23,408},{24,407},{35,420},{36,419},{47,432},{48... | collective-permute-start | bytes 6152 | tf_op jit(solution)/shard_map/ppermute | solution.py:492
  25.2 12.1 %collective-permute-start.2 = (f32[2,2560]{1,0:T(2,128)S(1)}, f32[2,2560]{1,0:T(2,128)S(1)}, u32[]{:S(2)}, u32[]{:S(2)}) collective-permute-start(f32[2,2560]{1,0:T(2,128)S(1)} %widen.1), channel_id=1, source_target_pairs={{0,384},{384,0},{1,385},{385,1},{2,386},{386,2},{3,387},{387,3},{4... | collective-permute-start | bytes 61448 | tf_op jit(solution)/shard_map/ppermute | solution.py:493
  32.8 4.4 %copy-start.1 = (s32[1,8,2048]{2,1,0:T(8,128)S(1)}, s32[1,8,2048]{2,1,0:T(8,128)}, u32[]{:S(2)}) copy-start(s32[1,8,2048]{2,1,0:T(8,128)} %param.11) | copy-start | bytes 196612
  32.8 4.4 %copy-start.2 = (f32[1,8,2048]{2,1,0:T(8,128)S(1)}, f32[1,8,2048]{2,1,0:T(8,128)}, u32[]{:S(2)}) copy-start(f32[1,8,2048]{2,1,0:T(8,128)} %param.12) | copy-start | bytes 196612
  32.9 4.4 %copy-start.6 = (f32[1,2]{1,0:T(1,128)S(1)}, f32[1,2]{1,0:T(1,128)}, u32[]{:S(2)}) copy-start(f32[1,2]{1,0:T(1,128)} %relax.1) | copy-start | bytes 28

commit v4 on v3

--- a/solution.py
+++ b/solution.py
@@ -435,7 +435,7 @@
         tiles[field, :, EDGE : EDGE + CORE] = core[rows, :]
         tiles[field, :, EDGE + CORE :] = ends[rows, EDGE:]
         before, value = tiles[field, 0:1, :], found_all[field : field + 1, :]
-        tiles[field, 0:1, :] = before + jnp.where(act[...] > 0, relax[0, field] * (value - before), 0.0)
+        tiles[field, 0:1, :] = before + jnp.where(act[...] > 0, relax[0:1, field : field + 1] * (value - before), 0.0)
         copy = pltpu.make_async_copy(
             tiles.at[field], out.at[pl.ds(LEV * field, 8), :], sems.at[2 * NF + 1 + field]
         )
@@ -452,7 +452,7 @@
             jax.ShapeDtypeStruct((NF, COLS), jnp.float32),
             jax.ShapeDtypeStruct((ROWS, COLS), jnp.float32),
         ),
-        in_specs=[VMEM, VMEM, VMEM, VMEM, VMEM, pl.BlockSpec(memory_space=pltpu.SMEM), VMEM, VMEM, ANY],
+        in_specs=[VMEM, VMEM, VMEM, VMEM, VMEM, VMEM, VMEM, VMEM, ANY],
         out_specs=(ANY, ANY),
         scratch_shapes=[
             pltpu.VMEM((NF, MID), jnp.float32),

time: 39.6 us -> 39.1 us (0.987)
  Pallas kernels: 9.09 us -> 8.55 us
    pallas_call x1, Pallas kernels: 1.61 us -> 1.06 us  [couple(): pl.pallas_call(couple_kernel, out_shape=(jax.ShapeDtypeStruct((NF, COLS),...]
where the time goes in v4:
time: 39.1 us; the launch traced here: 38.3 us
  starting transfers between devices  26.1 us (67%)
  Pallas kernels  8.55 us (22%)
  waiting for transfers between devices  1.52 us (4%)
  local copies, waits for them, and re-layouts  1.3 us (3%)
  between operations  0.81 us (2%)
    ppermute x1, starting transfers between devices, body(): far = lax.ppermute(far, 'col', long)  11.6 us
    ppermute x1, starting transfers between devices, body(): lax.ppermute(widen(chip, rim(near), surface), 'comp', [(0, 1), (1, 0)])  7.65 us
    pallas_call x1, Pallas kernels, inside(): pl.pallas_call(inside_kernel, out_shape=INNER + (jax.ShapeDtypeStruct((NF...  4.52 us
    ppermute x1, starting transfers between devices, body(): beyond = lax.ppermute(edge, ('comp', 'col'), across)  4.31 us
    pallas_call x1, Pallas kernels, advance(): pl.pallas_call(advance_kernel, out_shape=(jax.ShapeDtypeStruct((ROWS, COL...  2.86 us
    ppermute x1, starting transfers between devices, body(): chip = lax.ppermute(chip, 'col', same_chip)  1.92 us
    ppermute x1, waiting for transfers between devices, body(): lax.ppermute(widen(chip, rim(near), surface), 'comp', [(0, 1), (1, 0)])  1.51 us
    unnamed x14, local copies, waits for them, and re-layouts  1.3 us
  transfers between devices with their start and end apart: 5, of which 1 were waited for; matrix products, arithmetic and copies ran while one was open for 0% of the time, Pallas kernels for 19%

profile of v4, /device:TPU:6, one launch (start us, length us, event | category | flops | bytes accessed | tf_op | source)
XLA Modules:
  0.0 38.3 jit_solution(3698233070305131712)
XLA Ops:
  0.6 0.0 copy-start
  0.6 0.0 copy-start.3
  0.7 0.0 copy-start.4
  0.7 0.0 copy-start.5
  0.7 1.3 %copy-done = f32[1,2,80,2048]{3,2,1,0:T(8,128)S(1)} copy-done((f32[1,2,80,2048]{3,2,1,0:T(8,128)S(1)}, f32[1,2,80,2048]{3,2,1,0:T(8,128)}, u32[]{:S(2)}) %copy-start) | copy-done | bytes 1310744
  1.9 0.0 copy-done.3
  2.0 0.0 copy-done.4
  2.0 0.0 copy-done.5
  2.0 0.1 pack.1
  2.0 1.9 %collective-permute-start = (f32[168,512]{1,0:T(8,128)S(1)}, f32[168,512]{1,0:T(8,128)S(1)}, u32[]{:S(2)}, u32[]{:S(2)}) collective-permute-start(f32[168,512]{1,0:T(8,128)S(1)} %get-tuple-element.16), channel_id=1, source_target_pairs={{0,1},{1,0},{2,3},{3,2},{4,5},{5,4},{6,7},{7,6},{8,9},{9,8},{10,11... | collective-permute-start | bytes 1032200 | tf_op jit(solution)/shard_map/ppermute | solution.py:488
  4.0 0.7 %collective-permute-start.1 = (f32[168,512]{1,0:T(8,128)S(1)}, f32[168,512]{1,0:T(8,128)S(1)}, u32[]{:S(2)}, u32[]{:S(2)}) collective-permute-start(f32[168,512]{1,0:T(8,128)S(1)} %get-tuple-element.17), channel_id=1, source_target_pairs={{1,2},{2,1},{3,4},{4,3},{5,6},{6,5},{7,8},{8,7},{9,10},{10,9},{13,... | collective-permute-start | bytes 1032200 | tf_op jit(solution)/shard_map/ppermute | solution.py:489
  4.6 4.5 %inside.1 = (bf16[8,768,512]{2,1,0:T(8,128)(2,1)S(1)}, f32[160,1536]{1,0:T(8,128)S(1)}, bf16[320,1536]{1,0:T(8,128)(2,1)S(1)}, f32[160,1024]{1,0:T(8,128)S(1)}, ...) custom-call(f32[160,2048]{1,0:T(8,128)S(1)} %bitcast.8, s32[6,16,128]{2,1,0:T(8,128)S(1)} %bitcast.13, ...), custom_call_target="tpu_custom_call" | custom-call | flops 2000000000 | bytes 4000000 | tf_op jit(solution)/shard_map/inside/pallas_call | solution.py:256
  9.2 11.6 %collective-permute-start.4 = (f32[168,512]{1,0:T(8,128)S(1)}, f32[168,512]{1,0:T(8,128)S(1)}, u32[]{:S(2)}, u32[]{:S(2)}) collective-permute-start(f32[168,512]{1,0:T(8,128)S(1)} %get-tuple-element.20), channel_id=1, source_target_pairs={{11,12},{12,11},{23,24},{24,23},{35,36},{36,35},{47,48},{48,47},{5... | collective-permute-start | bytes 1032200 | tf_op jit(solution)/shard_map/ppermute | solution.py:491
  20.8 4.3 %collective-permute-start.3 = (f32[2,256]{1,0:T(2,128)S(1)}, f32[2,256]{1,0:T(2,128)S(1)}, u32[]{:S(2)}, u32[]{:S(2)}) collective-permute-start(f32[2,256]{1,0:T(2,128)S(1)} %get-tuple-element.19), channel_id=1, source_target_pairs={{11,396},{12,395},{23,408},{24,407},{35,420},{36,419},{47,432},{48... | collective-permute-start | bytes 6152 | tf_op jit(solution)/shard_map/ppermute | solution.py:492
  25.1 0.0 collective-permute-done.1.near
  25.1 0.0 collective-permute-done.chip
  25.2 7.6 %collective-permute-start.2 = (f32[2,2560]{1,0:T(2,128)S(1)}, f32[2,2560]{1,0:T(2,128)S(1)}, u32[]{:S(2)}, u32[]{:S(2)}) collective-permute-start(f32[2,2560]{1,0:T(2,128)S(1)} %widen.1), channel_id=1, source_target_pairs={{0,384},{384,0},{1,385},{385,1},{2,386},{386,2},{3,387},{387,3},{4... | collective-permute-start | bytes 61448 | tf_op jit(solution)/shard_map/ppermute | solution.py:493
  32.8 0.0 collective-permute-done.4.far
  32.8 0.0 copy-start.1
  32.8 0.0 copy-start.2
  32.9 0.0 copy-start.6
  32.9 2.9 %advance.1 = (f32[160,2048]{1,0:T(8,128)}, f32[160,1024]{1,0:T(8,128)S(1)}, f32[160,1024]{1,0:T(8,128)S(1)}) custom-call(f32[160,2048]{1,0:T(8,128)S(1)} %bitcast.9, f32[168,512]{1,0:T(8,128)S(1)} %collective-permute-done.chip, f32[168,512]{1,0:T(8,128)S(1)} %collective-permute-done.1.near, f32[168,512]{1,0:T(8,128)S(1)} %collective-permute-done.4.far, ...), custom_call_target="tpu_custom_call" | custom-call | flops 6000000000 | bytes 4000000 | tf_op jit(solution)/shard_map/advance/pallas_call | solution.py:365
  35.7 0.0 collective-permute-done.3.beyond
  35.7 1.5 %collective-permute-done.2.got = f32[2,2560]{1,0:T(2,128)S(1)} collective-permute-done((f32[2,2560]{1,0:T(2,128)S(1)}, f32[2,2560]{1,0:T(2,128)S(1)}, u32[]{:S(2)}, u32[]{:S(2)}) %collective-permute-start.2) | collective-permute-done | bytes 20512 | tf_op jit(solution)/shard_map/ppermute | solution.py:493
  37.2 0.0 copy-done.1
  37.2 0.0 copy-done.2
  37.3 0.0 copy-done.6
  37.3 1.1 %couple.1 = (f32[2,2048]{1,0:T(2,128)}, f32[160,2048]{1,0:T(8,128)}) custom-call(f32[2,2560]{1,0:T(2,128)S(1)} %collective-permute-done.2.got, f32[2,256]{1,0:T(2,128)S(1)} %collective-permute-done.3.beyond, s32[8,2048]{1,0:T(8,128)S(1)} %bitcast.10, f32[8,2048]{1,0:T(8,128)S(1)} %bitcast.11, ...), custom_call_target="tpu_custom_call", output_to_operand_aliasing={{1}: (8, {})} | custom-call | tf_op jit(solution)/shard_map/couple/pallas_call | solution.py:449
  (3 shorter events, 0.0 us)
Async XLA Ops:
  0.6 1.3 %copy-start = (f32[1,2,80,2048]{3,2,1,0:T(8,128)S(1)}, f32[1,2,80,2048]{3,2,1,0:T(8,128)}, u32[]{:S(2)}) copy-start(f32[1,2,80,2048]{3,2,1,0:T(8,128)} %param.7) | copy-start | bytes 3932164
  0.6 1.3 %copy-start.3 = (s32[1,6,2048]{2,0,1:T(1,128)S(1)}, s32[1,6,2048]{2,0,1:T(1,128)}, u32[]{:S(2)}) copy-start(s32[1,6,2048]{2,0,1:T(1,128)} %param.8) | copy-start | bytes 147460
  0.7 1.3 %copy-start.4 = (f32[1,6,2048]{2,0,1:T(1,128)S(1)}, f32[1,6,2048]{2,0,1:T(1,128)}, u32[]{:S(2)}) copy-start(f32[1,6,2048]{2,0,1:T(1,128)} %param.9) | copy-start | bytes 147460
  0.7 1.3 %copy-start.5 = (s32[1,2048]{1,0:T(1,128)S(1)}, s32[1,2048]{1,0:T(1,128)}, u32[]{:S(2)}) copy-start(s32[1,2048]{1,0:T(1,128)} %act.7) | copy-start | bytes 24580
  2.0 23.1 %collective-permute-start = (f32[168,512]{1,0:T(8,128)S(1)}, f32[168,512]{1,0:T(8,128)S(1)}, u32[]{:S(2)}, u32[]{:S(2)}) collective-permute-start(f32[168,512]{1,0:T(8,128)S(1)} %get-tuple-element.16), channel_id=1, source_target_pairs={{0,1},{1,0},{2,3},{3,2},{4,5},{5,4},{6,7},{7,6},{8,9},{9,8},{10,11... | collective-permute-start | bytes 1032200 | tf_op jit(solution)/shard_map/ppermute | solution.py:488
  4.0 21.1 %collective-permute-start.1 = (f32[168,512]{1,0:T(8,128)S(1)}, f32[168,512]{1,0:T(8,128)S(1)}, u32[]{:S(2)}, u32[]{:S(2)}) collective-permute-start(f32[168,512]{1,0:T(8,128)S(1)} %get-tuple-element.17), channel_id=1, source_target_pairs={{1,2},{2,1},{3,4},{4,3},{5,6},{6,5},{7,8},{8,7},{9,10},{10,9},{13,... | collective-permute-start | bytes 1032200 | tf_op jit(solution)/shard_map/ppermute | solution.py:489
  9.2 23.6 %collective-permute-start.4 = (f32[168,512]{1,0:T(8,128)S(1)}, f32[168,512]{1,0:T(8,128)S(1)}, u32[]{:S(2)}, u32[]{:S(2)}) collective-permute-start(f32[168,512]{1,0:T(8,128)S(1)} %get-tuple-element.20), channel_id=1, source_target_pairs={{11,12},{12,11},{23,24},{24,23},{35,36},{36,35},{47,48},{48,47},{5... | collective-permute-start | bytes 1032200 | tf_op jit(solution)/shard_map/ppermute | solution.py:491
  20.8 15.0 %collective-permute-start.3 = (f32[2,256]{1,0:T(2,128)S(1)}, f32[2,256]{1,0:T(2,128)S(1)}, u32[]{:S(2)}, u32[]{:S(2)}) collective-permute-start(f32[2,256]{1,0:T(2,128)S(1)} %get-tuple-element.19), channel_id=1, source_target_pairs={{11,396},{12,395},{23,408},{24,407},{35,420},{36,419},{47,432},{48... | collective-permute-start | bytes 6152 | tf_op jit(solution)/shard_map/ppermute | solution.py:492
  25.2 12.1 %collective-permute-start.2 = (f32[2,2560]{1,0:T(2,128)S(1)}, f32[2,2560]{1,0:T(2,128)S(1)}, u32[]{:S(2)}, u32[]{:S(2)}) collective-permute-start(f32[2,2560]{1,0:T(2,128)S(1)} %widen.1), channel_id=1, source_target_pairs={{0,384},{384,0},{1,385},{385,1},{2,386},{386,2},{3,387},{387,3},{4... | collective-permute-start | bytes 61448 | tf_op jit(solution)/shard_map/ppermute | solution.py:493
  32.8 4.4 %copy-start.1 = (s32[1,8,2048]{2,1,0:T(8,128)S(1)}, s32[1,8,2048]{2,1,0:T(8,128)}, u32[]{:S(2)}) copy-start(s32[1,8,2048]{2,1,0:T(8,128)} %param.11) | copy-start | bytes 196612
  32.8 4.4 %copy-start.2 = (f32[1,8,2048]{2,1,0:T(8,128)S(1)}, f32[1,8,2048]{2,1,0:T(8,128)}, u32[]{:S(2)}) copy-start(f32[1,8,2048]{2,1,0:T(8,128)} %param.12) | copy-start | bytes 196612
  32.9 4.4 %copy-start.6 = (f32[1,2]{1,0:T(1,128)S(1)}, f32[1,2]{1,0:T(1,128)}, u32[]{:S(2)}) copy-start(f32[1,2]{1,0:T(1,128)} %relax.1) | copy-start | bytes 28
